TPU v7x, 32 devices: a whole 2x2x4 slice. The times are simulated.
32 devices in a mesh: metro: 2 (over y), region: 8 (over z, x), dest: 2 (over core).
Axes of the slice: x: 2, y: 2, z: 4, core: 2. Of those that a mesh axis runs over, the one named last changes fastest.
Arguments:
- transitions: bfloat16 [256, 6, 128, 128], P(('metro', 'region')), parts along dimension 0, may hold values from 0 to 0.6
- tile_cols: int32 [256, 6], P(('metro', 'region')), parts along dimension 0, may hold values from 0 to 19, as said below
- tile_count: int32 [256], P(('metro', 'region')), parts along dimension 0, may hold values from 1 to 6
- publish: int32 [16, 4, 128], P(('metro', 'region')), parts along dimension 0, may hold values from 0 to 2047
- reward: float32 [32768], P(('metro', 'region')), parts along dimension 0, may hold values from -1 to 0
- value_init: bfloat16 [32768, 256], P(('metro', 'region'), 'dest'), parts along dimension 0, may hold values from -3 to 3
- anchor: bfloat16 [32768, 256], P(('metro', 'region'), 'dest'), parts along dimension 0, may hold values from 0.0009994507 to 0.0099487305
- goal_segment_index: int32 [512], P(('metro', 'dest')), parts along dimension 0, may hold values from 0 to 16383
- routes: int32 [512, 64], P(('metro', 'dest')), parts along dimension 0, may hold values from 0 to 16383
Outputs:
- reward_grad: float32 [32768], P(('metro', 'region', 'dest')), parts along dimension 0
There are 2 independent parts, one for each index of `metro`. A program takes and returns all parts, laid end to end along the dimension named above; each array names one. Nothing has to cross between parts.
Inputs may be any that keep to these rules, and one draw needn't show every extreme that they name: `tile_cols`: tile 0 of every block row names one of the region's own blocks (a value under 16); values 16 + j name the boundary block of offset j; tiles at k >= tile_count of their block row are padding with arbitrary contents.
All inputs are finite; a program needn't handle non-finite values.
Results may differ from a plain program's by a relative error of at most 0.0003.
Values may be sent and summed in bfloat16 or wider, within the bound.
A program may use at most 64 MiB of HBM per device.

v0:
```python
import jax
import jax.numpy as jnp
from jax import lax
from jax.sharding import PartitionSpec as P

OFFSETS = (-2, -1, 1, 2)


def shifted(value, axis, by):
    size = lax.axis_size(axis)
    pairs = [(i, i + by) for i in range(size) if 0 <= i + by < size]
    return lax.ppermute(value, axis, pairs)


def body(
    transitions,
    tile_cols,
    tile_count,
    publish,
    reward,
    value_init,
    anchor,
    goal_segment_index,
    routes,
):
    blocks_dev = transitions.shape[0]
    kmax_dev = transitions.shape[1]
    tile_rows = transitions.shape[2]
    local_segments = blocks_dev * tile_rows
    goal_width = anchor.shape[1]
    first_seg = lax.axis_index("region") * local_segments
    columns_all = blocks_dev + 4
    live_mask = lax.broadcasted_iota(jnp.int32, (blocks_dev, kmax_dev), 1) < tile_count[:, None]
    fold_target = jnp.where(live_mask, tile_cols, columns_all)
    column_iota = lax.broadcasted_iota(jnp.int32, (blocks_dev, kmax_dev, columns_all), 2)
    fold_hot = (fold_target[:, :, None] == column_iota).astype(jnp.float32)
    fold_hot_bf16 = fold_hot.astype(jnp.bfloat16)
    published = publish[0].reshape(-1)
    seg_iota = lax.broadcasted_iota(jnp.int32, (published.shape[0], local_segments), 1)
    pub_hot = (published[:, None] == seg_iota).astype(jnp.float32)
    pub_hot_bf16 = pub_hot.astype(jnp.bfloat16)
    segment_index = first_seg + lax.broadcasted_iota(jnp.int32, (local_segments, goal_width), 0)
    leaving_reward = (segment_index == goal_segment_index[None, :]).astype(jnp.float32)

    def incoming(zfield):
        selected = jnp.dot(pub_hot_bf16, zfield, preferred_element_type=jnp.float32)
        pieces = selected.astype(jnp.bfloat16).reshape(4, tile_rows, goal_width)
        arrived = [None, None, None, None]
        for slot_index, offset in enumerate(OFFSETS):
            arrived[slot_index] = shifted(pieces[slot_index], "region", -offset)
        own_blocks = zfield.reshape(blocks_dev, tile_rows, goal_width)
        return jnp.concatenate([own_blocks, jnp.stack(arrived)], 0)

    def outgoing(parts):
        arrived = [None, None, None, None]
        for slot_index, offset in enumerate(OFFSETS):
            arrived[slot_index] = shifted(
                parts[slot_index].astype(jnp.bfloat16), "region", offset
            ).astype(jnp.float32)
        return arrived

    def backup(zfield):
        extended = incoming(zfield)
        picked = jnp.einsum(
            "bkc,cjd->bkjd", fold_hot_bf16, extended, preferred_element_type=jnp.float32
        ).astype(jnp.bfloat16)
        total_sum = jnp.einsum(
            "bkij,bkjd->bid", transitions, picked, preferred_element_type=jnp.float32
        )
        return reward[:, None] + jnp.log(
            total_sum.reshape(local_segments, goal_width) + leaving_reward
        )

    z_start = jnp.exp(value_init.astype(jnp.float32)).astype(jnp.bfloat16)
    value_one = backup(z_start)
    z_one = jnp.exp(value_one).astype(jnp.bfloat16)
    value_two = backup(z_one)
    weight_rows = jnp.exp(reward[:, None] - value_two)
    anchor_flow = anchor.astype(jnp.float32)
    z_factor = z_one.astype(jnp.float32)

    def sweep(flow):
        weighted = (
            (flow * weight_rows).astype(jnp.bfloat16).reshape(blocks_dev, tile_rows, goal_width)
        )
        contrib = jnp.einsum(
            "bkij,bid->bkjd", transitions, weighted, preferred_element_type=jnp.float32
        )
        folded = jnp.einsum("bkc,bkjd->cjd", fold_hot, contrib, precision=lax.Precision.HIGHEST)
        local_flow = folded[:blocks_dev].reshape(local_segments, goal_width)
        arrived = outgoing(folded[blocks_dev:])
        stacked = jnp.stack(arrived).reshape(4 * tile_rows, goal_width)
        local_flow = local_flow + jnp.einsum(
            "ps,pd->sd", pub_hot, stacked, precision=lax.Precision.HIGHEST
        )
        return anchor_flow + z_factor * local_flow

    flow_one = sweep(anchor_flow)
    flow_two = sweep(flow_one)
    visits = anchor_flow + flow_one + flow_two
    route_ids = (routes - first_seg).reshape(-1)
    id_total = route_ids.shape[0]
    block_width = 1024
    id_blocks = route_ids.reshape(id_total // block_width, block_width)
    row_iota = lax.broadcasted_iota(jnp.int32, (local_segments, block_width), 0)

    def count_block(id_row):
        return jnp.sum((id_row[None, :] == row_iota).astype(jnp.float32), axis=1)

    route_total = jnp.sum(lax.map(count_block, id_blocks), axis=0)
    local_terms = route_total - jnp.sum(visits, axis=1)
    summed_all = lax.psum(local_terms, "dest")
    share_rows = local_segments // lax.axis_size("dest")
    return lax.dynamic_slice_in_dim(summed_all, lax.axis_index("dest") * share_rows, share_rows)


def solution(mesh):
    return jax.shard_map(
        body,
        mesh=mesh,
        in_specs=(
            P(("metro", "region"), None, None, None),
            P(("metro", "region"), None),
            P(("metro", "region")),
            P(("metro", "region"), None, None),
            P(("metro", "region")),
            P(("metro", "region"), "dest"),
            P(("metro", "region"), "dest"),
            P(("metro", "dest")),
            P(("metro", "dest"), None),
        ),
        out_specs=P(("metro", "region", "dest")),
        check_vma=False,
    )
```

profile of v0, /device:TPU:0, one launch (start us, length us, event | category | flops | bytes accessed | tf_op | source)
XLA Modules:
  0.0 129.8 jit_solution(14647911259363348517)
XLA Ops:
  0.0 2.0 %fusion.22 = bf16[512,128]{1,0:T(8,128)(2,1)S(1)} fusion(s32[512]{0:T(512)} %bitcast.165, bf16[2048,128]{1,0:T(8,128)(2,1)} %param.16), kind=kOutput, calls=%fused_computation.36 | convolution fusion | flops 272171008 | bytes 657408 | tf_op jit(solution)/shard_map/dot_general | solution.py:46
  2.0 4.9 %collective-permute-start = (bf16[128,128]{1,0:T(8,128)(2,1)S(1)}, bf16[128,128]{1,0:T(8,128)(2,1)S(1)}, u32[]{:S(2)}, u32[]{:S(2)}) collective-permute-start(bf16[128,128]{1,0:T(8,128)(2,1)S(1)} %get-tuple-element.57), channel_id=1, source_target_pairs={{0,4},{2,6},{4,8},{6,10},{8,12},{10,14},{1,5},{3,7},{5,9},{7,11},{... | collective-permute-start | bytes 98312 | tf_op jit(solution)/shard_map/ppermute | solution.py:12
  6.9 3.4 %collective-permute-start.1 = (bf16[128,128]{1,0:T(8,128)(2,1)S(1)}, bf16[128,128]{1,0:T(8,128)(2,1)S(1)}, u32[]{:S(2)}, u32[]{:S(2)}) collective-permute-start(bf16[128,128]{1,0:T(8,128)(2,1)S(1)} %get-tuple-element.56), channel_id=1, source_target_pairs={{0,2},{2,4},{4,6},{6,8},{8,10},{10,12},{12,14},{1,3},{3,5},{5,7},{... | collective-permute-start | bytes 98312 | tf_op jit(solution)/shard_map/ppermute | solution.py:12
  14.0 2.2 %copy.77 = bf16[16,128,128]{2,0,1:T(8,128)(2,1)} copy(bf16[16,128,128]{2,1,0:T(8,128)(2,1)} %bitcast.138) | data formatting | bytes 1048576 | tf_op jit(solution)/shard_map/reshape | solution.py:51
  16.4 2.7 %collective-permute-done.3 = bf16[128,128]{1,0:T(8,128)(2,1)S(1)} collective-permute-done((bf16[128,128]{1,0:T(8,128)(2,1)S(1)}, bf16[128,128]{1,0:T(8,128)(2,1)S(1)}, u32[]{:S(2)}, u32[]{:S(2)}) %collective-permute-start.3) | collective-permute-done | bytes 32800 | tf_op jit(solution)/shard_map/ppermute | solution.py:12
  19.1 4.3 %concatenate.6 = bf16[20,128,128]{2,0,1:T(8,128)(2,1)} concatenate(bf16[16,128,128]{2,0,1:T(8,128)(2,1)} %copy.77, bf16[1,128,128]{2,0,1:T(2,128)(2,1)S(1)} %copy.78, bf16[1,128,128]{2,0,1:T(2,128)(2,1)S(1)} %copy.79, bf16[1,128,128]{2,0,1:T(2,128)(2,1)S(1)} %copy.80, bf16[1,128,128]{2,0,1:T(2,128)(2,1)S(1)} %copy.81), dimensions={0} | concatenate | bytes 1310720 | tf_op jit(solution)/shard_map/concatenate | solution.py:52
  23.4 2.2 %convolution_convert_fusion.1 = bf16[16,6,128,128]{3,0,2,1:T(8,128)(2,1)S(1)} fusion(bf16[20,128,128]{2,0,1:T(8,128)(2,1)} %concatenate.6, s32[16,6]{0,1:T(8,128)S(1)} %fusion.51), kind=kOutput, calls=%fused_computation.24 | convolution fusion | flops 64493184 | bytes 3801472 | tf_op jit(solution)/shard_map/bkc,cjd->bkjd/dot_general | solution.py:64
  25.6 2.2 %fusion.40 = (bf16[20,128,128]{2,1,0:T(8,128)(2,1)S(1)}, f32[16,128,128,1]{1,2,3,0:T(8,128)S(1)}) fusion(s32[128]{0:T(128)S(1)} %copy-done.13, s32[16,128]{1,0:T(8,128)S(1)} %add_add_fusion, f32[16,128]{1,0:T(8,128)S(1)} %bitcast.146, bf16[16,6,128,128]{3,2,1,0:T(8,128)(2,1)S(1)} %copy-done, bf16[16,6,128,128]{3,0,2,1:T(8,128)(2,1)S(1)} %convolution_convert_fusion.1), kind=kOutput, calls=%fused_computation.57 | convolution fusion | flops 403963904 | bytes 7881216 | tf_op jit(solution)/shard_map/bkij,bkjd->bid/dot_general | solution.py:67
  29.4 3.9 %collective-permute-start.4 = (bf16[128,128]{1,0:T(8,128)(2,1)S(1)}, bf16[128,128]{1,0:T(8,128)(2,1)S(1)}, u32[]{:S(2)}, u32[]{:S(2)}) collective-permute-start(bf16[128,128]{1,0:T(8,128)(2,1)S(1)} %get-tuple-element.53), channel_id=1, source_target_pairs={{0,4},{2,6},{4,8},{6,10},{8,12},{10,14},{1,5},{3,7},{5,9},{7,11},{... | collective-permute-start | bytes 98312 | tf_op jit(solution)/shard_map/ppermute | solution.py:12
  33.4 2.5 %collective-permute-start.5 = (bf16[128,128]{1,0:T(8,128)(2,1)S(1)}, bf16[128,128]{1,0:T(8,128)(2,1)S(1)}, u32[]{:S(2)}, u32[]{:S(2)}) collective-permute-start(bf16[128,128]{1,0:T(8,128)(2,1)S(1)} %get-tuple-element.52), channel_id=1, source_target_pairs={{0,2},{2,4},{4,6},{6,8},{8,10},{10,12},{12,14},{1,3},{3,5},{5,7},{... | collective-permute-start | bytes 98312 | tf_op jit(solution)/shard_map/ppermute | solution.py:12
  35.9 1.3 collective-permute-start.6
  37.2 1.5 %collective-permute-start.7 = (bf16[128,128]{1,0:T(8,128)(2,1)S(1)}, bf16[128,128]{1,0:T(8,128)(2,1)S(1)}, u32[]{:S(2)}, u32[]{:S(2)}) collective-permute-start(bf16[128,128]{1,0:T(8,128)(2,1)S(1)} %get-tuple-element.50), channel_id=1, source_target_pairs={{4,0},{6,2},{8,4},{10,6},{12,8},{14,10},{5,1},{7,3},{9,5},{11,7},{... | collective-permute-start | bytes 98312 | tf_op jit(solution)/shard_map/ppermute | solution.py:12
  38.7 3.4 %collective-permute-done.6 = bf16[128,128]{1,0:T(8,128)(2,1)S(1)} collective-permute-done((bf16[128,128]{1,0:T(8,128)(2,1)S(1)}, bf16[128,128]{1,0:T(8,128)(2,1)S(1)}, u32[]{:S(2)}, u32[]{:S(2)}) %collective-permute-start.6) | collective-permute-done | bytes 32800 | tf_op jit(solution)/shard_map/ppermute | solution.py:12
  42.1 3.4 %collective-permute-done.7 = bf16[128,128]{1,0:T(8,128)(2,1)S(1)} collective-permute-done((bf16[128,128]{1,0:T(8,128)(2,1)S(1)}, bf16[128,128]{1,0:T(8,128)(2,1)S(1)}, u32[]{:S(2)}, u32[]{:S(2)}) %collective-permute-start.7) | collective-permute-done | bytes 32800 | tf_op jit(solution)/shard_map/ppermute | solution.py:12
  46.6 1.9 %fusion.4 = f32[16,128,128,1]{1,2,3,0:T(8,128)S(1)} fusion(bf16[16,6,128,128]{3,2,1,0:T(8,128)(2,1)S(1)} %copy-done, bf16[16,6,128,128]{3,0,2,1:T(8,128)(2,1)S(1)} %convolution_convert_fusion), kind=kOutput, calls=%fused_computation.8 | convolution fusion | flops 402653184 | bytes 7340032 | tf_op jit(solution)/shard_map/bkij,bkjd->bid/dot_general | solution.py:67
  50.4 3.6 %convolution_bitcast_fusion.1 = f32[16,6,128,128]{2,3,1,0:T(8,128)} fusion(bf16[16,128,128,1]{2,1,3,0:T(8,128)(2,1)S(1)} %bitcast.137, bf16[16,6,128,128]{3,2,1,0:T(8,128)(2,1)S(1)} %copy-done), kind=kOutput, calls=%fused_computation.15 | convolution fusion | flops 402653184 | bytes 9961472 | tf_op jit(solution)/shard_map/bkij,bid->bkjd/dot_general | solution.py:86
  54.0 6.8 %copy.86 = f32[16,6,128,128]{3,0,1,2:T(8,128)} copy(f32[16,6,128,128]{2,3,1,0:T(8,128)} %convolution_bitcast_fusion.1) | data formatting | bytes 12582912 | tf_op jit(solution)/shard_map/bkij,bid->bkjd/dot_general | solution.py:86
  60.8 6.1 %fusion.56 = (bf16[20,128,128]{2,0,1:T(8,128)(2,1)S(1)}, f32[20,128,128]{2,0,1:T(8,128)}) fusion(f32[16,6,128,128]{3,0,1,2:T(8,128)} %copy.86, s32[16,6]{0,1:T(8,128)S(1)} %fusion.51), kind=kOutput, calls=%fused_computation.89 | convolution fusion | flops 377816960 | bytes 8257920 | tf_op jit(solution)/shard_map/bkc,bkjd->cjd/dot_general | solution.py:89
  69.8 5.2 %collective-permute-start.10 = (bf16[128,128]{1,0:T(8,128)(2,1)S(1)}, bf16[128,128]{1,0:T(8,128)(2,1)}, u32[]{:S(2)}, u32[]{:S(2)}) collective-permute-start(bf16[128,128]{1,0:T(8,128)(2,1)S(1)} %bitcast.157), channel_id=1, source_target_pairs={{0,2},{2,4},{4,6},{6,8},{8,10},{10,12},{12,14},{1,3},{3,5},{5,7},{... | collective-permute-start | bytes 98312 | tf_op jit(solution)/shard_map/ppermute | solution.py:12
  74.9 4.6 %collective-permute-start.11 = (bf16[128,128]{1,0:T(8,128)(2,1)S(1)}, bf16[128,128]{1,0:T(8,128)(2,1)}, u32[]{:S(2)}, u32[]{:S(2)}) collective-permute-start(bf16[128,128]{1,0:T(8,128)(2,1)S(1)} %bitcast.158), channel_id=1, source_target_pairs={{0,4},{2,6},{4,8},{6,10},{8,12},{10,14},{1,5},{3,7},{5,9},{7,11},{... | collective-permute-start | bytes 98312 | tf_op jit(solution)/shard_map/ppermute | solution.py:12
  79.7 1.5 %slice.106 = f32[16,128,128]{2,0,1:T(8,128)S(1)} slice(f32[20,128,128]{2,0,1:T(8,128)} %get-tuple-element.61), slice={[0:16], [0:128], [0:128]} | slice | bytes 2097152 | tf_op jit(solution)/shard_map/slice | solution.py:90
  82.4 2.8 %multiply_convert_fusion = (bf16[2048,128]{1,0:T(8,128)(2,1)S(1)}, f32[2048,128]{1,0:T(8,128)}) fusion(f32[16,128,128,1]{1,2,3,0:T(8,128)S(1)} %copy-done.2, s32[128]{0:T(128)S(1)} %copy-done.13, f32[2048]{0:T(1024)S(1)} %copy-done.10, s32[2048]{0:T(1024)S(1)} %iota_add_fusion, f32[2048,128]{1,0:T(8,128)S(1)} %bitcast.139, ...), kind=kOutput, calls=%fused_computation.52 | convolution fusion | flops 272629760 | bytes 4868608 | tf_op jit(solution)/shard_map/ps,pd->sd/dot_general | solution.py:93
  85.2 3.6 %convolution_bitcast_fusion = f32[16,6,128,128]{2,3,1,0:T(8,128)} fusion(bf16[16,128,128,1]{2,1,3,0:T(8,128)(2,1)S(1)} %bitcast.141, bf16[16,6,128,128]{3,2,1,0:T(8,128)(2,1)S(1)} %copy-done), kind=kOutput, calls=%fused_computation.14 | convolution fusion | flops 402653184 | bytes 9961472 | tf_op jit(solution)/shard_map/bkij,bid->bkjd/dot_general | solution.py:86
  88.9 6.8 %copy.89 = f32[16,6,128,128]{3,0,1,2:T(8,128)} copy(f32[16,6,128,128]{2,3,1,0:T(8,128)} %convolution_bitcast_fusion) | data formatting | bytes 12582912 | tf_op jit(solution)/shard_map/bkij,bid->bkjd/dot_general | solution.py:86
  95.7 6.1 %fusion.57 = (bf16[20,128,128]{2,0,1:T(8,128)(2,1)S(1)}, f32[20,128,128]{2,0,1:T(8,128)}) fusion(f32[16,6,128,128]{3,0,1,2:T(8,128)} %copy.89, s32[16,6]{0,1:T(8,128)S(1)} %fusion.51), kind=kOutput, calls=%fused_computation.90 | convolution fusion | flops 377816960 | bytes 8257920 | tf_op jit(solution)/shard_map/bkc,bkjd->cjd/dot_general | solution.py:89
  103.3 1.3 collective-permute-start.13
  104.6 4.5 %collective-permute-start.14 = (bf16[128,128]{1,0:T(8,128)(2,1)S(1)}, bf16[128,128]{1,0:T(8,128)(2,1)S(1)}, u32[]{:S(2)}, u32[]{:S(2)}) collective-permute-start(bf16[128,128]{1,0:T(8,128)(2,1)S(1)} %bitcast.149), channel_id=1, source_target_pairs={{0,2},{2,4},{4,6},{6,8},{8,10},{10,12},{12,14},{1,3},{3,5},{5,7},{... | collective-permute-start | bytes 98312 | tf_op jit(solution)/shard_map/ppermute | solution.py:12
  109.2 4.6 %collective-permute-start.15 = (bf16[128,128]{1,0:T(8,128)(2,1)S(1)}, bf16[128,128]{1,0:T(8,128)(2,1)S(1)}, u32[]{:S(2)}, u32[]{:S(2)}) collective-permute-start(bf16[128,128]{1,0:T(8,128)(2,1)S(1)} %bitcast.150), channel_id=1, source_target_pairs={{0,4},{2,6},{4,8},{6,10},{8,12},{10,14},{1,5},{3,7},{5,9},{7,11},{... | collective-permute-start | bytes 98312 | tf_op jit(solution)/shard_map/ppermute | solution.py:12
  113.8 9.3 %while.11 = (s32[]{:T(128)}, f32[8,2048]{1,0:T(8,128)S(1)}, s32[8,1024]{1,0:T(8,128)S(1)}, s32[]{:T(128)}, s32[]{:T(128)}) while((s32[]{:T(128)}, f32[8,2048]{1,0:T(8,128)S(1)}, s32[8,1024]{1,0:T(8,128)S(1)}, s32[]{:T(128)}, s32[]{:T(128)}) %tuple.37), condition=%wide.region_2.3_spmd.clone, body=%wide.region_0.2_spmd.clone.sunk | while | flops 6289410 | bytes 36933 | solution.py:110
  123.2 1.5 %slice.111 = f32[16,128,128]{2,0,1:T(8,128)S(1)} slice(f32[20,128,128]{2,0,1:T(8,128)} %get-tuple-element.65), slice={[0:16], [0:128], [0:128]} | slice | bytes 2097152 | tf_op jit(solution)/shard_map/slice | solution.py:90
  125.1 1.7 %fusion.21 = f32[2048]{0:T(1024)S(1)} fusion(f32[2048,128]{1,0:T(8,128)S(1)} %bitcast.140, bf16[512,128]{1,0:T(8,128)(2,1)S(1)} %bitcast.144, s32[512]{0:T(512)S(1)} %bitcast.168, bf16[2048,128]{1,0:T(8,128)(2,1)S(1)} %copy-done.9, bf16[2048,128]{1,0:T(8,128)(2,1)S(1)} %copy-done.5, f32[2048,128]{1,0:T(8,128)S(1)} %copy-done.16), kind=kOutput, calls=%fused_computation.35 | convolution fusion | flops 271579136 | bytes 3287040 | tf_op jit(solution)/shard_map/ps,pd->sd/dot_general | solution.py:93
  126.7 2.5 %psum.7 = f32[2048]{0:T(1024)S(1)} all-reduce(f32[2048]{0:T(1024)S(1)} %sub.18), channel_id=1, replica_groups=mesh['metro'=2,'region'=8,'dest'=2] {'dest'}, use_global_device_ids=true, to_apply=%region_5.6 | all-reduce | flops 2048 | bytes 16384 | tf_op jit(solution)/shard_map/psum | solution.py:112
  (115 shorter events, 24.1 us)
Async XLA Ops:
  0.0 25.5 %copy-start = (bf16[16,6,128,128]{3,2,1,0:T(8,128)(2,1)S(1)}, bf16[16,6,128,128]{3,2,1,0:T(8,128)(2,1)}, u32[]{:S(2)}) copy-start(bf16[16,6,128,128]{3,2,1,0:T(8,128)(2,1)} %param.11) | copy-start | bytes 9437188
  0.0 12.9 %copy-start.6 = (bf16[2048,128]{1,0:T(8,128)(2,1)S(1)}, bf16[2048,128]{1,0:T(8,128)(2,1)}, u32[]{:S(2)}) copy-start(bf16[2048,128]{1,0:T(8,128)(2,1)} %param.16) | copy-start | bytes 1572868
  0.0 13.9 %copy-start.12 = (s32[16,6]{0,1:T(8,128)S(1)}, s32[16,6]{0,1:T(8,128)}, u32[]{:S(2)}) copy-start(s32[16,6]{0,1:T(8,128)} %param.12) | copy-start | bytes 1156
  0.0 13.9 %copy-start.14 = (s32[16]{0:T(128)S(1)}, s32[16]{0:T(128)}, u32[]{:S(2)}) copy-start(s32[16]{0:T(128)} %param.13) | copy-start | bytes 196
  2.0 14.2 %collective-permute-start = (bf16[128,128]{1,0:T(8,128)(2,1)S(1)}, bf16[128,128]{1,0:T(8,128)(2,1)S(1)}, u32[]{:S(2)}, u32[]{:S(2)}) collective-permute-start(bf16[128,128]{1,0:T(8,128)(2,1)S(1)} %get-tuple-element.57), channel_id=1, source_target_pairs={{0,4},{2,6},{4,8},{6,10},{8,12},{10,14},{1,5},{3,7},{5,9},{7,11},{... | collective-permute-start | bytes 98312 | tf_op jit(solution)/shard_map/ppermute | solution.py:12
  6.9 9.3 %collective-permute-start.1 = (bf16[128,128]{1,0:T(8,128)(2,1)S(1)}, bf16[128,128]{1,0:T(8,128)(2,1)S(1)}, u32[]{:S(2)}, u32[]{:S(2)}) collective-permute-start(bf16[128,128]{1,0:T(8,128)(2,1)S(1)} %get-tuple-element.56), channel_id=1, source_target_pairs={{0,2},{2,4},{4,6},{6,8},{8,10},{10,12},{12,14},{1,3},{3,5},{5,7},{... | collective-permute-start | bytes 98312 | tf_op jit(solution)/shard_map/ppermute | solution.py:12
  10.3 6.0 %collective-permute-start.2 = (bf16[128,128]{1,0:T(8,128)(2,1)S(1)}, bf16[128,128]{1,0:T(8,128)(2,1)S(1)}, u32[]{:S(2)}, u32[]{:S(2)}) collective-permute-start(bf16[128,128]{1,0:T(8,128)(2,1)S(1)} %get-tuple-element.55), channel_id=1, source_target_pairs={{2,0},{4,2},{6,4},{8,6},{10,8},{12,10},{14,12},{3,1},{5,3},{7,5},{... | collective-permute-start | bytes 98312 | tf_op jit(solution)/shard_map/ppermute | solution.py:12
  11.6 7.4 %collective-permute-start.3 = (bf16[128,128]{1,0:T(8,128)(2,1)S(1)}, bf16[128,128]{1,0:T(8,128)(2,1)S(1)}, u32[]{:S(2)}, u32[]{:S(2)}) collective-permute-start(bf16[128,128]{1,0:T(8,128)(2,1)S(1)} %get-tuple-element.54), channel_id=1, source_target_pairs={{4,0},{6,2},{8,4},{10,6},{12,8},{14,10},{5,1},{7,3},{9,5},{11,7},{... | collective-permute-start | bytes 98312 | tf_op jit(solution)/shard_map/ppermute | solution.py:12
  16.2 9.4 %copy-start.10 = (f32[2048]{0:T(1024)S(1)}, f32[2048]{0:T(1024)}, u32[]{:S(2)}) copy-start(f32[2048]{0:T(1024)} %param.15) | copy-start | bytes 24580
  16.2 9.4 %copy-start.13 = (s32[128]{0:T(128)S(1)}, s32[128]{0:T(128)}, u32[]{:S(2)}) copy-start(s32[128]{0:T(128)} %param.18) | copy-start | bytes 1540
  25.6 3.1 %copy-start.15 = (s32[1,4,128]{2,1,0:T(4,128)S(1)}, s32[1,4,128]{2,1,0:T(4,128)}, u32[]{:S(2)}) copy-start(s32[1,4,128]{2,1,0:T(4,128)} %param.14) | copy-start | bytes 6148
  28.7 16.9 %copy-start.7 = (bf16[2048,128]{1,0:T(8,128)(2,1)}, bf16[2048,128]{1,0:T(8,128)(2,1)S(1)}, u32[]{:S(2)}) copy-start(bf16[2048,128]{1,0:T(8,128)(2,1)S(1)} %fusion.27) | copy-start | bytes 1572868
  29.4 9.2 %collective-permute-start.4 = (bf16[128,128]{1,0:T(8,128)(2,1)S(1)}, bf16[128,128]{1,0:T(8,128)(2,1)S(1)}, u32[]{:S(2)}, u32[]{:S(2)}) collective-permute-start(bf16[128,128]{1,0:T(8,128)(2,1)S(1)} %get-tuple-element.53), channel_id=1, source_target_pairs={{0,4},{2,6},{4,8},{6,10},{8,12},{10,14},{1,5},{3,7},{5,9},{7,11},{... | collective-permute-start | bytes 98312 | tf_op jit(solution)/shard_map/ppermute | solution.py:12
  33.4 5.3 %collective-permute-start.5 = (bf16[128,128]{1,0:T(8,128)(2,1)S(1)}, bf16[128,128]{1,0:T(8,128)(2,1)S(1)}, u32[]{:S(2)}, u32[]{:S(2)}) collective-permute-start(bf16[128,128]{1,0:T(8,128)(2,1)S(1)} %get-tuple-element.52), channel_id=1, source_target_pairs={{0,2},{2,4},{4,6},{6,8},{8,10},{10,12},{12,14},{1,3},{3,5},{5,7},{... | collective-permute-start | bytes 98312 | tf_op jit(solution)/shard_map/ppermute | solution.py:12
  35.9 6.3 %collective-permute-start.6 = (bf16[128,128]{1,0:T(8,128)(2,1)S(1)}, bf16[128,128]{1,0:T(8,128)(2,1)S(1)}, u32[]{:S(2)}, u32[]{:S(2)}) collective-permute-start(bf16[128,128]{1,0:T(8,128)(2,1)S(1)} %get-tuple-element.51), channel_id=1, source_target_pairs={{2,0},{4,2},{6,4},{8,6},{10,8},{12,10},{14,12},{3,1},{5,3},{7,5},{... | collective-permute-start | bytes 98312 | tf_op jit(solution)/shard_map/ppermute | solution.py:12
  37.2 8.3 %collective-permute-start.7 = (bf16[128,128]{1,0:T(8,128)(2,1)S(1)}, bf16[128,128]{1,0:T(8,128)(2,1)S(1)}, u32[]{:S(2)}, u32[]{:S(2)}) collective-permute-start(bf16[128,128]{1,0:T(8,128)(2,1)S(1)} %get-tuple-element.50), channel_id=1, source_target_pairs={{4,0},{6,2},{8,4},{10,6},{12,8},{14,10},{5,1},{7,3},{9,5},{11,7},{... | collective-permute-start | bytes 98312 | tf_op jit(solution)/shard_map/ppermute | solution.py:12
  46.6 3.0 %copy-start.3 = (bf16[2048,128]{1,0:T(8,128)(2,1)S(1)}, bf16[2048,128]{1,0:T(8,128)(2,1)}, u32[]{:S(2)}) copy-start(bf16[2048,128]{1,0:T(8,128)(2,1)} %param.17) | copy-start | bytes 1572868
  60.8 18.7 %copy-start.11 = (s32[128,64]{0,1:T(8,128)S(1)}, s32[128,64]{0,1:T(8,128)}, u32[]{:S(2)}) copy-start(s32[128,64]{0,1:T(8,128)} %param.19) | copy-start | bytes 98308
  67.1 14.4 %collective-permute-start.8 = (bf16[128,128]{1,0:T(8,128)(2,1)S(1)}, bf16[128,128]{1,0:T(8,128)(2,1)S(1)}, u32[]{:S(2)}, u32[]{:S(2)}) collective-permute-start(bf16[128,128]{1,0:T(8,128)(2,1)S(1)} %bitcast.153), channel_id=1, source_target_pairs={{4,0},{6,2},{8,4},{10,6},{12,8},{14,10},{5,1},{7,3},{9,5},{11,7},{... | collective-permute-start | bytes 98312 | tf_op jit(solution)/shard_map/ppermute | solution.py:12
  68.4 13.1 %collective-permute-start.9 = (bf16[128,128]{1,0:T(8,128)(2,1)S(1)}, bf16[128,128]{1,0:T(8,128)(2,1)S(1)}, u32[]{:S(2)}, u32[]{:S(2)}) collective-permute-start(bf16[128,128]{1,0:T(8,128)(2,1)S(1)} %bitcast.155), channel_id=1, source_target_pairs={{2,0},{4,2},{6,4},{8,6},{10,8},{12,10},{14,12},{3,1},{5,3},{7,5},{... | collective-permute-start | bytes 98312 | tf_op jit(solution)/shard_map/ppermute | solution.py:12
  69.8 11.8 %collective-permute-start.10 = (bf16[128,128]{1,0:T(8,128)(2,1)S(1)}, bf16[128,128]{1,0:T(8,128)(2,1)}, u32[]{:S(2)}, u32[]{:S(2)}) collective-permute-start(bf16[128,128]{1,0:T(8,128)(2,1)S(1)} %bitcast.157), channel_id=1, source_target_pairs={{0,2},{2,4},{4,6},{6,8},{8,10},{10,12},{12,14},{1,3},{3,5},{5,7},{... | collective-permute-start | bytes 98312 | tf_op jit(solution)/shard_map/ppermute | solution.py:12
  74.9 6.6 %collective-permute-start.11 = (bf16[128,128]{1,0:T(8,128)(2,1)S(1)}, bf16[128,128]{1,0:T(8,128)(2,1)}, u32[]{:S(2)}, u32[]{:S(2)}) collective-permute-start(bf16[128,128]{1,0:T(8,128)(2,1)S(1)} %bitcast.158), channel_id=1, source_target_pairs={{0,4},{2,6},{4,8},{6,10},{8,12},{10,14},{1,5},{3,7},{5,9},{7,11},{... | collective-permute-start | bytes 98312 | tf_op jit(solution)/shard_map/ppermute | solution.py:12
  79.7 2.7 %copy-start.2 = (f32[16,128,128,1]{1,2,3,0:T(8,128)S(1)}, f32[16,128,128,1]{1,2,3,0:T(8,128)}, u32[]{:S(2)}) copy-start(f32[16,128,128,1]{1,2,3,0:T(8,128)} %copy-done.1) | copy-start | bytes 3145732
  79.7 2.7 %copy-start.4 = (bf16[2048,128]{1,0:T(8,128)(2,1)S(1)}, bf16[2048,128]{1,0:T(8,128)(2,1)}, u32[]{:S(2)}) copy-start(bf16[2048,128]{1,0:T(8,128)(2,1)} %param.17) | copy-start | bytes 1572868
  79.7 2.7 %copy-start.8 = (bf16[2048,128]{1,0:T(8,128)(2,1)S(1)}, bf16[2048,128]{1,0:T(8,128)(2,1)}, u32[]{:S(2)}) copy-start(bf16[2048,128]{1,0:T(8,128)(2,1)} %copy-done.7) | copy-start | bytes 1572868
  102.0 23.0 %collective-permute-start.12 = (bf16[128,128]{1,0:T(8,128)(2,1)S(1)}, bf16[128,128]{1,0:T(8,128)(2,1)S(1)}, u32[]{:S(2)}, u32[]{:S(2)}) collective-permute-start(bf16[128,128]{1,0:T(8,128)(2,1)S(1)} %bitcast.147), channel_id=1, source_target_pairs={{4,0},{6,2},{8,4},{10,6},{12,8},{14,10},{5,1},{7,3},{9,5},{11,7},{... | collective-permute-start | bytes 98312 | tf_op jit(solution)/shard_map/ppermute | solution.py:12
  103.3 21.7 %collective-permute-start.13 = (bf16[128,128]{1,0:T(8,128)(2,1)S(1)}, bf16[128,128]{1,0:T(8,128)(2,1)S(1)}, u32[]{:S(2)}, u32[]{:S(2)}) collective-permute-start(bf16[128,128]{1,0:T(8,128)(2,1)S(1)} %bitcast.148), channel_id=1, source_target_pairs={{2,0},{4,2},{6,4},{8,6},{10,8},{12,10},{14,12},{3,1},{5,3},{7,5},{... | collective-permute-start | bytes 98312 | tf_op jit(solution)/shard_map/ppermute | solution.py:12
  104.6 20.4 %collective-permute-start.14 = (bf16[128,128]{1,0:T(8,128)(2,1)S(1)}, bf16[128,128]{1,0:T(8,128)(2,1)S(1)}, u32[]{:S(2)}, u32[]{:S(2)}) collective-permute-start(bf16[128,128]{1,0:T(8,128)(2,1)S(1)} %bitcast.149), channel_id=1, source_target_pairs={{0,2},{2,4},{4,6},{6,8},{8,10},{10,12},{12,14},{1,3},{3,5},{5,7},{... | collective-permute-start | bytes 98312 | tf_op jit(solution)/shard_map/ppermute | solution.py:12
  109.2 15.8 %collective-permute-start.15 = (bf16[128,128]{1,0:T(8,128)(2,1)S(1)}, bf16[128,128]{1,0:T(8,128)(2,1)S(1)}, u32[]{:S(2)}, u32[]{:S(2)}) collective-permute-start(bf16[128,128]{1,0:T(8,128)(2,1)S(1)} %bitcast.150), channel_id=1, source_target_pairs={{0,4},{2,6},{4,8},{6,10},{8,12},{10,14},{1,5},{3,7},{5,9},{7,11},{... | collective-permute-start | bytes 98312 | tf_op jit(solution)/shard_map/ppermute | solution.py:12
  123.1 1.9 %copy-start.5 = (bf16[2048,128]{1,0:T(8,128)(2,1)S(1)}, bf16[2048,128]{1,0:T(8,128)(2,1)}, u32[]{:S(2)}) copy-start(bf16[2048,128]{1,0:T(8,128)(2,1)} %param.17) | copy-start | bytes 1572868
  123.1 1.9 %copy-start.9 = (bf16[2048,128]{1,0:T(8,128)(2,1)S(1)}, bf16[2048,128]{1,0:T(8,128)(2,1)}, u32[]{:S(2)}) copy-start(bf16[2048,128]{1,0:T(8,128)(2,1)} %copy-done.7) | copy-start | bytes 1572868
  123.2 1.9 %copy-start.16 = (f32[2048,128]{1,0:T(8,128)S(1)}, f32[2048,128]{1,0:T(8,128)}, u32[]{:S(2)}) copy-start(f32[2048,128]{1,0:T(8,128)} %get-tuple-element.63) | copy-start | bytes 3145732
  (1 other events, 1.0 us)
where the time goes:
time: 131 us; the launch traced here: 130 us
  starting transfers between devices  44.1 us (34%)
  matrix products  34.1 us (26%)
  local copies, waits for them, and re-layouts  27.8 us (21%)
  other arithmetic  10.8 us (8%)
  waiting for transfers between devices  9.51 us (7%)
  blocking collectives  2.5 us (2%)
    ppermute x16, starting transfers between devices, shifted(): return lax.ppermute(value, axis, pairs)  44.1 us
    dot_general x2, local copies, waits for them, and re-layouts, sweep(): jnp.einsum('bkij,bid->bkjd', transitions, weighted, preferred_element_typ...  13.5 us
    dot_general x2, matrix products, sweep(): jnp.einsum('bkc,bkjd->cjd', fold_hot, contrib, precision=lax.Precision.HI...  12.3 us
    ppermute x16, waiting for transfers between devices, shifted(): return lax.ppermute(value, axis, pairs)  9.51 us
    reduce_sum x8, other arithmetic, count_block(): return jnp.sum((id_row[None, :] == row_iota).astype(jnp.float32), axis=1)  7.36 us
    dot_general x2, matrix products, sweep(): jnp.einsum('bkij,bid->bkjd', transitions, weighted, preferred_element_typ...  7.3 us
    dot_general x2, matrix products, sweep(): jnp.einsum('ps,pd->sd', pub_hot, stacked, precision=lax.Precision.HIGHEST)  4.5 us
    concatenate x2, local copies, waits for them, and re-layouts, incoming(): return jnp.concatenate([own_blocks, jnp.stack(arrived)], 0)  4.26 us
  transfers between devices with their start and end apart: 16, of which 3 were waited for; matrix products, arithmetic and copies ran while one was open for 13% of the time, Pallas kernels for 0%

commit v1 on v0

v1 whole, which is shorter than its diff:
```python
import functools

import jax
import jax.numpy as jnp
from jax import lax
from jax.experimental import pallas as pl
from jax.experimental.pallas import tpu as pltpu
from jax.sharding import PartitionSpec as P

OFFSETS = (-2, -1, 1, 2)
MESH = pl.DeviceIdType.MESH
F32 = jnp.float32
BF16 = jnp.bfloat16
LAST = (((1,), (1,)), ((), ()))


def dims(blocks, kmax):
    tiles = blocks * kmax
    cols = blocks + 4
    pairs = (tiles + cols) // 2
    return tiles, cols, pairs


def plan(tile_cols, tile_count):
    blocks, kmax = tile_cols.shape
    tiles, cols, pairs = dims(blocks, kmax)
    live = lax.broadcasted_iota(jnp.int32, (blocks, kmax), 1) < tile_count[:, None]
    col = jnp.where(live, tile_cols, cols).reshape(tiles)
    tile = jnp.arange(tiles, dtype=jnp.int32)
    cid = jnp.arange(cols, dtype=jnp.int32)
    same = col[:, None] == col[None, :]
    rank = jnp.sum((same & (tile[None, :] < tile[:, None])).astype(jnp.int32), 1)
    count = jnp.sum((col[:, None] == cid[None, :]).astype(jnp.int32), 0)
    padded = (count + 1) // 2 * 2
    start = jnp.sum(jnp.where(cid[None, :] < cid[:, None], padded[None, :], 0), 1)
    first = jnp.sum(jnp.where(cid[None, :] < col[:, None], padded[None, :], 0), 1)
    spot = jnp.where(col < cols, first + rank, -1)
    slot = jnp.arange(2 * pairs, dtype=jnp.int32)
    hit = slot[:, None] == spot[None, :]
    tile_at = jnp.sum(jnp.where(hit, tile[None, :], 0), 1)
    block_at = blocks + jnp.sum(jnp.where(hit, (tile // kmax - blocks)[None, :], 0), 1)
    pair = jnp.arange(pairs, dtype=jnp.int32)
    fresh = jnp.any((pair[:, None] * 2 == start[None, :]) & (count[None, :] > 0), 1)
    keep = 1 - fresh.astype(jnp.int32)
    last = jnp.where(count > 0, (start + padded) // 2 - 1, pairs)
    return jnp.concatenate([col, tile_at, block_at, keep, last])


def kernel(
    shape,
    lists,
    publish,
    reward,
    goal,
    routes,
    trans_hbm,
    init_hbm,
    anchor_hbm,
    out,
    trans,
    init,
    anchor_in,
    anchor,
    ext1,
    ext2,
    piece1,
    piece2,
    hot,
    ids,
    gap,
    inv,
    flow_u,
    sums,
    part1,
    part2,
    arr1,
    arr2,
    total,
    other,
    load_sem,
    send_sem,
    recv_sem,
    dest_sem,
):
    blocks, kmax, regions = shape
    tiles, cols, pairs = dims(blocks, kmax)
    tile = 128
    me = lax.axis_index("region")
    side = lax.axis_index("dest")
    first_seg = me * (blocks * tile)
    at_tile, at_block = tiles, tiles + 2 * pairs
    at_keep = tiles + 4 * pairs
    at_last = at_keep + pairs

    load_init = pltpu.make_async_copy(init_hbm, init, load_sem.at[0])
    load_trans = pltpu.make_async_copy(trans_hbm, trans, load_sem.at[1])
    load_anchor = pltpu.make_async_copy(anchor_hbm, anchor_in, load_sem.at[2])
    load_init.start()
    load_trans.start()
    load_anchor.start()

    def inside(by):
        return (me + by >= 0) & (me + by < regions)

    barrier = pltpu.get_barrier_semaphore()
    pl.semaphore_signal(barrier, inc=1, device_id={"dest": 1 - side}, device_id_type=MESH)
    for by in OFFSETS:
        @pl.when(inside(by))
        def _():
            pl.semaphore_signal(barrier, inc=1, device_id={"region": me + by}, device_id_type=MESH)

    zero = jnp.zeros((tile, tile), BF16)
    ext1[cols] = zero
    ext2[cols] = zero
    flow_u[blocks] = zero
    sums[pairs] = jnp.zeros((tile, tile), F32)
    for j, by in enumerate(OFFSETS):
        @pl.when(jnp.logical_not(inside(by)))
        def _():
            ext1[blocks + j] = zero
            ext2[blocks + j] = zero

        @pl.when(jnp.logical_not(inside(-by)))
        def _():
            arr1[j] = zero
            arr2[j] = zero

    row = lax.broadcasted_iota(jnp.int32, (tile, tile), 0)
    lane = lax.broadcasted_iota(jnp.int32, (tile, tile), 1)

    def make_hot(c, carry):
        for j in range(4):
            pub = publish[j : j + 1, :]
            hit = (row + c * tile) == pub
            hot[j, pl.ds(pl.multiple_of(c * tile, tile), tile), :] = jnp.where(hit, 1.0, 0.0).astype(BF16)
        return carry

    lax.fori_loop(0, blocks, make_hot, 0)

    load_init.wait()

    def make_start(b, carry):
        block = init[pl.ds(pl.multiple_of(b * tile, tile), tile), :].astype(F32)
        ext1[b] = jnp.exp(block.T).astype(BF16)
        return carry

    lax.fori_loop(0, blocks, make_start, 0, unroll=2)

    def exchange(phase, source, target, base, sign):
        def copy(j):
            return pltpu.make_async_remote_copy(
                src_ref=source.at[j],
                dst_ref=target.at[base + j],
                send_sem=send_sem.at[phase, j],
                recv_sem=recv_sem.at[phase, j],
                device_id={"region": me + sign * OFFSETS[j]},
                device_id_type=MESH,
            )

        def start(j):
            @pl.when(inside(sign * OFFSETS[j]))
            def _():
                copy(j).start()

        def wait():
            for j in range(4):
                @pl.when(inside(-sign * OFFSETS[j]))
                def _():
                    copy(j).wait_recv()

        def finish():
            for j in range(4):
                @pl.when(inside(sign * OFFSETS[j]))
                def _():
                    copy(j).wait_send()

        return start, wait, finish

    def publish_rows(ext, piece, start):
        whole = jnp.concatenate([ext[b] for b in range(blocks)], 1)
        for j in range(4):
            picked = jnp.dot(whole, hot[j], preferred_element_type=F32)
            piece[j] = picked.astype(BF16)
            start(j)

    def product(ext, b):
        left = jnp.concatenate([ext[lists[b * kmax + k]] for k in range(kmax)], 1)
        right = jnp.concatenate([trans[b * kmax + k] for k in range(kmax)], 1)
        return lax.dot_general(left, right, LAST, preferred_element_type=F32)

    def bonus(b):
        return jnp.where(gap[...] == b * tile, 1.0, 0.0)

    neighbours = 1
    for by in OFFSETS:
        neighbours = neighbours + inside(by).astype(jnp.int32)
    pl.semaphore_wait(barrier, neighbours)

    start1, wait1, finish1 = exchange(0, piece1, ext1, blocks, -1)
    start2, wait2, finish2 = exchange(1, piece2, ext2, blocks, -1)
    start3, wait3, finish3 = exchange(2, part1, arr1, 0, 1)
    start4, wait4, finish4 = exchange(3, part2, arr2, 0, 1)

    publish_rows(ext1, piece1, start1)

    gap[...] = jnp.broadcast_to(goal[...] - first_seg, (tile, tile)).T - lane
    ids[...] = (routes[...] - first_seg).T
    group = 4

    def count(q, acc):
        highs, lows = [], []
        for g in range(group):
            line = ids[pl.ds(q * group + g, 1), :]
            low = jnp.bitwise_and(line, tile - 1)
            high = lax.shift_right_arithmetic(line, 7)
            lows.append(jnp.where(row == low, 1.0, 0.0).astype(BF16))
            highs.append(jnp.where(row[:blocks] == high, 1.0, 0.0).astype(BF16))
        return acc + lax.dot_general(
            jnp.concatenate(highs, 1), jnp.concatenate(lows, 1), LAST, preferred_element_type=F32
        )

    total[...] = lax.fori_loop(0, ids.shape[0] // group, count, jnp.zeros((blocks, tile), F32))

    load_trans.wait()
    wait1()

    def first_backup(b, carry):
        y = product(ext1, b) + bonus(b)
        ext2[b] = (jnp.exp(reward[pl.ds(b, 1), :]) * y).astype(BF16)
        return carry

    lax.fori_loop(0, blocks, first_backup, 0, unroll=2)
    publish_rows(ext2, piece2, start2)

    load_anchor.wait()

    def turn(b, carry):
        anchor[b] = anchor_in[pl.ds(pl.multiple_of(b * tile, tile), tile), :].astype(F32).T
        return carry

    lax.fori_loop(0, blocks, turn, 0, unroll=2)
    wait2()

    def second_backup(b, carry):
        y = product(ext2, b) + bonus(b)
        w = 1.0 / y
        inv[b] = w
        flow_u[b] = (anchor[b] * w).astype(BF16)
        return carry

    lax.fori_loop(0, blocks, second_backup, 0, unroll=2)

    def spread(part, start):
        def step(t, acc):
            left = jnp.concatenate(
                [flow_u[lists[at_block + 2 * t + h]] for h in range(2)], 1
            )
            right = jnp.concatenate([trans[lists[at_tile + 2 * t + h]] for h in range(2)], 0)
            new = jnp.dot(left, right, preferred_element_type=F32)
            acc = acc * lists[at_keep + t].astype(F32) + new
            sums[t] = acc
            return acc

        lax.fori_loop(0, pairs, step, jnp.zeros((tile, tile), F32), unroll=2)
        for j in range(4):
            part[j] = sums[lists[at_last + blocks + j]].astype(BF16)
            start(j)

    def arrive(arr, c):
        left = jnp.concatenate([arr[j] for j in range(4)], 1)
        rows = pl.ds(pl.multiple_of(c * tile, tile), tile)
        right = jnp.concatenate([hot[j, rows, :] for j in range(4)], 1)
        back = lax.dot_general(left, right, LAST, preferred_element_type=F32)
        local = sums[lists[at_last + c]] + back
        return anchor[c] + ext2[c].astype(F32) * local

    spread(part1, start3)
    wait3()

    def first_flow(c, carry):
        flow = arrive(arr1, c)
        flow_u[c] = (flow * inv[c]).astype(BF16)
        here = pl.ds(c, 1)
        total[here, :] = total[here, :] - jnp.sum(anchor[c] + flow, axis=0, keepdims=True)
        return carry

    lax.fori_loop(0, blocks, first_flow, 0, unroll=2)
    spread(part2, start4)
    wait4()

    def second_flow(c, carry):
        flow = arrive(arr2, c)
        here = pl.ds(c, 1)
        total[here, :] = total[here, :] - jnp.sum(flow, axis=0, keepdims=True)
        return carry

    lax.fori_loop(0, blocks, second_flow, 0, unroll=2)

    share = blocks // 2
    mine = pl.ds(pl.multiple_of(side * share, share), share)
    theirs = pl.ds(pl.multiple_of((1 - side) * share, share), share)
    swap = pltpu.make_async_remote_copy(
        src_ref=total.at[theirs],
        dst_ref=other,
        send_sem=dest_sem.at[0],
        recv_sem=dest_sem.at[1],
        device_id={"dest": 1 - side},
        device_id_type=MESH,
    )
    swap.start()
    finish1()
    finish2()
    finish3()
    finish4()
    swap.wait()
    out[...] = total[mine, :] + other[...]


def body(
    regions,
    transitions,
    tile_cols,
    tile_count,
    publish,
    reward,
    value_init,
    anchor,
    goal_segment_index,
    routes,
):
    blocks, kmax, tile, _ = transitions.shape
    width = anchor.shape[1]
    tiles, cols, pairs = dims(blocks, kmax)
    lists = plan(tile_cols, tile_count)
    vmem = pl.BlockSpec(memory_space=pltpu.VMEM)
    smem = pl.BlockSpec(memory_space=pltpu.SMEM)
    hbm = pl.BlockSpec(memory_space=pl.ANY)
    out = pl.pallas_call(
        functools.partial(kernel, (blocks, kmax, regions)),
        out_shape=jax.ShapeDtypeStruct((blocks // 2, tile), F32),
        in_specs=[smem, vmem, vmem, vmem, vmem, hbm, hbm, hbm],
        out_specs=vmem,
        scratch_shapes=[
            pltpu.VMEM((tiles, tile, tile), BF16),
            pltpu.VMEM((blocks * tile, width), BF16),
            pltpu.VMEM((blocks * tile, width), BF16),
            pltpu.VMEM((blocks, width, tile), F32),
            pltpu.VMEM((cols + 1, width, tile), BF16),
            pltpu.VMEM((cols + 1, width, tile), BF16),
            pltpu.VMEM((4, width, tile), BF16),
            pltpu.VMEM((4, width, tile), BF16),
            pltpu.VMEM((4, blocks * tile, tile), BF16),
            pltpu.VMEM((routes.shape[1], routes.shape[0]), jnp.int32),
            pltpu.VMEM((width, tile), jnp.int32),
            pltpu.VMEM((blocks, width, tile), F32),
            pltpu.VMEM((blocks + 1, width, tile), BF16),
            pltpu.VMEM((pairs + 1, width, tile), F32),
            pltpu.VMEM((4, width, tile), BF16),
            pltpu.VMEM((4, width, tile), BF16),
            pltpu.VMEM((4, width, tile), BF16),
            pltpu.VMEM((4, width, tile), BF16),
            pltpu.VMEM((blocks, tile), F32),
            pltpu.VMEM((blocks // 2, tile), F32),
            pltpu.SemaphoreType.DMA((3,)),
            pltpu.SemaphoreType.DMA((4, 4)),
            pltpu.SemaphoreType.DMA((4, 4)),
            pltpu.SemaphoreType.DMA((2,)),
        ],
        compiler_params=pltpu.CompilerParams(
            collective_id=0, has_side_effects=True, vmem_limit_bytes=40 * 1024 * 1024
        ),
    )(
        lists,
        publish[0],
        reward.reshape(blocks, tile),
        goal_segment_index.reshape(1, width),
        routes,
        transitions.reshape(tiles, tile, tile),
        value_init,
        anchor,
    )
    return out.reshape(-1)


def solution(mesh):
    return jax.shard_map(
        functools.partial(body, mesh.shape["region"]),
        mesh=mesh,
        in_specs=(
            P(("metro", "region"), None, None, None),
            P(("metro", "region"), None),
            P(("metro", "region")),
            P(("metro", "region"), None, None),
            P(("metro", "region")),
            P(("metro", "region"), "dest"),
            P(("metro", "region"), "dest"),
            P(("metro", "dest")),
            P(("metro", "dest"), None),
        ),
        out_specs=P(("metro", "region", "dest")),
        check_vma=False,
    )
```

time: 131 us -> 49.8 us (0.38)
  starting transfers between devices: 44.1 us -> 0 us
  Pallas kernels: 0 us -> 40.1 us
  matrix products: 34.1 us -> 0 us
  local copies, waits for them, and re-layouts: 27.8 us -> 7.7 us
  waiting for transfers between devices: 9.51 us -> 0 us
  other arithmetic: 10.8 us -> 1.45 us
  blocking collectives: 2.5 us -> 0 us
    ppermute x16 -> x0, starting transfers between devices: 44.1 us -> none  [shifted(): return lax.ppermute(value, axis, pairs)]
    pallas_call x0 -> x1, Pallas kernels: none -> 40.1 us  [body(): pl.pallas_call(functools.partial(kernel, (blocks, kmax, regions)), out_sh...]
    dot_general x12 -> x0, matrix products: 34.1 us -> none  [the longest x2 12.3 us: sweep(): jnp.einsum('bkc,bkjd->cjd', fold_hot, contrib, precision=lax.Precision.HI...]
    dot_general x2 -> x0, local copies, waits for them, and re-layouts: 13.5 us -> none  [sweep(): jnp.einsum('bkij,bid->bkjd', transitions, weighted, preferred_element_typ...]
    ppermute x16 -> x0, waiting for transfers between devices: 9.51 us -> none  [shifted(): return lax.ppermute(value, axis, pairs)]
    reduce_sum x9 -> x5, other arithmetic: 7.39 us -> 0.59 us  [the longest x1 0.17 us: plan(): jnp.sum((same & (tile[None, :] < tile[:, None])).astype(jnp.int32), 1)]
    unnamed x45 -> x14, local copies, waits for them, and re-layouts: 1.16 us -> 7.45 us
    concatenate x2 -> x1, local copies, waits for them, and re-layouts: 4.26 us -> 0.08 us  [plan(): return jnp.concatenate([col, tile_at, block_at, keep, last])]
  transfers between devices with their start and end apart: 16 -> 0, of which waited for: 3 -> 0; matrix products, arithmetic and copies ran while one was open for 13% -> 0% of each run, Pallas kernels for 0% -> 0%
where the time goes in v1:
time: 49.8 us; the launch traced here: 49.4 us
  Pallas kernels  40.1 us (81%)
  local copies, waits for them, and re-layouts  7.7 us (15%)
  other arithmetic  1.45 us (3%)
    pallas_call x1, Pallas kernels, body(): pl.pallas_call(functools.partial(kernel, (blocks, kmax, regions)), out_sh...  40.1 us
    unnamed x14, local copies, waits for them, and re-layouts  7.45 us

profile of v1, /device:TPU:0, one launch (start us, length us, event | category | flops | bytes accessed | tf_op | source)
XLA Modules:
  0.0 49.4 jit_solution(10534549238605132749)
XLA Ops:
  0.0 0.7 %fusion.1 = s32[16,6]{0,1:T(8,128)S(1)} fusion(s32[16,6]{0,1:T(8,128)} %param.10, s32[16]{0:T(128)} %param.11), kind=kLoop, calls=%fused_computation.14 | loop fusion | flops 192 | bytes 832 | tf_op jit(solution)/shard_map/jit(_where)/select_n | solution.py:28
  0.7 0.1 copy.14
  0.8 0.1 reshape.72
  0.9 0.1 convert_reduce_fusion.1
  1.0 0.1 select_reduce_fusion.2
  1.1 0.1 select_reduce_fusion.3
  1.3 0.1 and_reduce_fusion
  1.4 0.2 convert_reduce_fusion
  1.6 0.1 select_reduce_fusion
  1.7 0.1 concatenate.3.lists
  1.8 0.8 %copy.15.routes = s32[128,64]{1,0:T(8,128)S(1)} copy(s32[128,64]{0,1:T(8,128)} %param.17) | data formatting | bytes 65536 | tf_op args[8]
  2.6 0.0 copy-start
  2.6 1.9 %copy-done = bf16[16,6,128,128]{3,2,1,0:T(8,128)(2,1)S(1)} copy-done((bf16[16,6,128,128]{3,2,1,0:T(8,128)(2,1)S(1)}, bf16[16,6,128,128]{3,2,1,0:T(8,128)(2,1)}, u32[]{:S(2)}) %copy-start) | copy-done | bytes 3145752
  4.5 0.0 copy-start.1
  4.5 1.0 %copy-done.1 = bf16[2048,128]{1,0:T(8,128)(2,1)S(1)} copy-done((bf16[2048,128]{1,0:T(8,128)(2,1)S(1)}, bf16[2048,128]{1,0:T(8,128)(2,1)}, u32[]{:S(2)}) %copy-start.1) | copy-done | bytes 524312
  5.5 0.0 copy-start.2
  5.5 1.0 %copy-done.2 = bf16[2048,128]{1,0:T(8,128)(2,1)S(1)} copy-done((bf16[2048,128]{1,0:T(8,128)(2,1)S(1)}, bf16[2048,128]{1,0:T(8,128)(2,1)}, u32[]{:S(2)}) %copy-start.2) | copy-done | bytes 524312
  6.6 0.0 copy-start.3
  6.6 0.7 %copy-done.3 = f32[2048]{0:T(1024)S(1)} copy-done((f32[2048]{0:T(1024)S(1)}, f32[2048]{0:T(1024)}, u32[]{:S(2)}) %copy-start.3) | copy-done | bytes 8216
  7.3 0.0 copy-start.4
  7.3 0.7 %copy-done.4 = s32[1,4,128]{2,1,0:T(4,128)S(1)} copy-done((s32[1,4,128]{2,1,0:T(4,128)S(1)}, s32[1,4,128]{2,1,0:T(4,128)}, u32[]{:S(2)}) %copy-start.4) | copy-done | bytes 2072
  8.0 0.0 copy-start.5
  8.0 0.7 %copy-done.5 = s32[128]{0:T(128)S(1)} copy-done((s32[128]{0:T(128)S(1)}, s32[128]{0:T(128)}, u32[]{:S(2)}) %copy-start.5) | copy-done | bytes 536
  8.6 40.1 %shard_map.91 = f32[8,128]{1,0:T(8,128)S(1)} custom-call(s32[406]{0:T(512)S(1)} %concatenate.3.lists, s32[4,128]{1,0:T(4,128)S(1)} %bitcast.8, f32[16,128]{1,0:T(8,128)S(1)} %bitcast.7, s32[1,128]{1,0:T(1,128)S(1)} %bitcast.9, s32[128,64]{1,0:T(8,128)S(1)} %copy.15.routes, bf16[96,128,128]{2,1,0:T(8,128)(2,1)S(1)} %bitcast.5, ...), custom_call_target="tpu_custom_call" | custom-call | tf_op jit(solution)/shard_map/pallas_call | solution.py:338
  48.8 0.6 %copy.17 = f32[1024]{0:T(1024)} copy(f32[1024]{0:T(1024)S(1)} %bitcast.6) | data formatting | bytes 8192
  (7 shorter events, 0.1 us)
Async XLA Ops:
  2.6 1.9 %copy-start = (bf16[16,6,128,128]{3,2,1,0:T(8,128)(2,1)S(1)}, bf16[16,6,128,128]{3,2,1,0:T(8,128)(2,1)}, u32[]{:S(2)}) copy-start(bf16[16,6,128,128]{3,2,1,0:T(8,128)(2,1)} %param.9) | copy-start | bytes 9437188
  4.5 1.0 %copy-start.1 = (bf16[2048,128]{1,0:T(8,128)(2,1)S(1)}, bf16[2048,128]{1,0:T(8,128)(2,1)}, u32[]{:S(2)}) copy-start(bf16[2048,128]{1,0:T(8,128)(2,1)} %init_hbm.1) | copy-start | bytes 1572868
  5.5 1.0 %copy-start.2 = (bf16[2048,128]{1,0:T(8,128)(2,1)S(1)}, bf16[2048,128]{1,0:T(8,128)(2,1)}, u32[]{:S(2)}) copy-start(bf16[2048,128]{1,0:T(8,128)(2,1)} %anchor_hbm.1) | copy-start | bytes 1572868
  6.6 0.7 %copy-start.3 = (f32[2048]{0:T(1024)S(1)}, f32[2048]{0:T(1024)}, u32[]{:S(2)}) copy-start(f32[2048]{0:T(1024)} %param.13) | copy-start | bytes 24580
  7.3 0.7 %copy-start.4 = (s32[1,4,128]{2,1,0:T(4,128)S(1)}, s32[1,4,128]{2,1,0:T(4,128)}, u32[]{:S(2)}) copy-start(s32[1,4,128]{2,1,0:T(4,128)} %param.12) | copy-start | bytes 6148
  8.0 0.7 %copy-start.5 = (s32[128]{0:T(128)S(1)}, s32[128]{0:T(128)}, u32[]{:S(2)}) copy-start(s32[128]{0:T(128)} %param.16) | copy-start | bytes 1540

commit v2 on v1

--- a/solution.py
+++ b/solution.py
@@ -135,7 +135,7 @@
             hot[j, pl.ds(pl.multiple_of(c * tile, tile), tile), :] = jnp.where(hit, 1.0, 0.0).astype(BF16)
         return carry
 
-    lax.fori_loop(0, blocks, make_hot, 0)
+    lax.fori_loop(0, blocks, make_hot, 0, unroll=True)
 
     load_init.wait()
 
@@ -144,7 +144,7 @@
         ext1[b] = jnp.exp(block.T).astype(BF16)
         return carry
 
-    lax.fori_loop(0, blocks, make_start, 0, unroll=2)
+    lax.fori_loop(0, blocks, make_start, 0, unroll=True)
 
     def exchange(phase, source, target, base, sign):
         def copy(j):
@@ -204,7 +204,7 @@
     publish_rows(ext1, piece1, start1)
 
     gap[...] = jnp.broadcast_to(goal[...] - first_seg, (tile, tile)).T - lane
-    ids[...] = (routes[...] - first_seg).T
+    ids[...] = routes[...] - first_seg
     group = 4
 
     def count(q, acc):
@@ -219,7 +219,7 @@
             jnp.concatenate(highs, 1), jnp.concatenate(lows, 1), LAST, preferred_element_type=F32
         )
 
-    total[...] = lax.fori_loop(0, ids.shape[0] // group, count, jnp.zeros((blocks, tile), F32))
+    total[...] = lax.fori_loop(0, ids.shape[0] // group, count, jnp.zeros((blocks, tile), F32), unroll=True)
 
     load_trans.wait()
     wait1()
@@ -229,7 +229,7 @@
         ext2[b] = (jnp.exp(reward[pl.ds(b, 1), :]) * y).astype(BF16)
         return carry
 
-    lax.fori_loop(0, blocks, first_backup, 0, unroll=2)
+    lax.fori_loop(0, blocks, first_backup, 0, unroll=True)
     publish_rows(ext2, piece2, start2)
 
     load_anchor.wait()
@@ -238,7 +238,7 @@
         anchor[b] = anchor_in[pl.ds(pl.multiple_of(b * tile, tile), tile), :].astype(F32).T
         return carry
 
-    lax.fori_loop(0, blocks, turn, 0, unroll=2)
+    lax.fori_loop(0, blocks, turn, 0, unroll=True)
     wait2()
 
     def second_backup(b, carry):
@@ -248,7 +248,7 @@
         flow_u[b] = (anchor[b] * w).astype(BF16)
         return carry
 
-    lax.fori_loop(0, blocks, second_backup, 0, unroll=2)
+    lax.fori_loop(0, blocks, second_backup, 0, unroll=True)
 
     def spread(part, start):
         def step(t, acc):
@@ -261,7 +261,7 @@
             sums[t] = acc
             return acc
 
-        lax.fori_loop(0, pairs, step, jnp.zeros((tile, tile), F32), unroll=2)
+        lax.fori_loop(0, pairs, step, jnp.zeros((tile, tile), F32), unroll=True)
         for j in range(4):
             part[j] = sums[lists[at_last + blocks + j]].astype(BF16)
             start(j)
@@ -284,7 +284,7 @@
         total[here, :] = total[here, :] - jnp.sum(anchor[c] + flow, axis=0, keepdims=True)
         return carry
 
-    lax.fori_loop(0, blocks, first_flow, 0, unroll=2)
+    lax.fori_loop(0, blocks, first_flow, 0, unroll=True)
     spread(part2, start4)
     wait4()
 
@@ -294,7 +294,7 @@
         total[here, :] = total[here, :] - jnp.sum(flow, axis=0, keepdims=True)
         return carry
 
-    lax.fori_loop(0, blocks, second_flow, 0, unroll=2)
+    lax.fori_loop(0, blocks, second_flow, 0, unroll=True)
 
     share = blocks // 2
     mine = pl.ds(pl.multiple_of(side * share, share), share)
@@ -334,7 +334,7 @@
     lists = plan(tile_cols, tile_count)
     vmem = pl.BlockSpec(memory_space=pltpu.VMEM)
     smem = pl.BlockSpec(memory_space=pltpu.SMEM)
-    hbm = pl.BlockSpec(memory_space=pl.ANY)
+    hbm = pl.BlockSpec(memory_space=pltpu.HBM)
     out = pl.pallas_call(
         functools.partial(kernel, (blocks, kmax, regions)),
         out_shape=jax.ShapeDtypeStruct((blocks // 2, tile), F32),
@@ -367,14 +367,14 @@
             pltpu.SemaphoreType.DMA((2,)),
         ],
         compiler_params=pltpu.CompilerParams(
-            collective_id=0, has_side_effects=True, vmem_limit_bytes=40 * 1024 * 1024
+            collective_id=0, has_side_effects=True, vmem_limit_bytes=56 * 1024 * 1024
         ),
     )(
         lists,
         publish[0],
         reward.reshape(blocks, tile),
         goal_segment_index.reshape(1, width),
-        routes,
+        routes.T,
         transitions.reshape(tiles, tile, tile),
         value_init,
         anchor,

time: 49.8 us -> 32.2 us (0.65)
  Pallas kernels: 40.1 us -> 28.3 us
  local copies, waits for them, and re-layouts: 7.7 us -> 2.11 us
    pallas_call x1, Pallas kernels: 40.1 us -> 28.3 us  [body(): pl.pallas_call(functools.partial(kernel, (blocks, kmax, regions)), out_sh...]
    unnamed x14 -> x1, local copies, waits for them, and re-layouts: 7.45 us -> 1.28 us
    concatenate x1, local copies, waits for them, and re-layouts: 0.08 us -> 0.66 us  [plan(): return jnp.concatenate([col, tile_at, block_at, keep, last])]
where the time goes in v2:
time: 32.2 us; the launch traced here: 31.9 us
  Pallas kernels  28.3 us (88%)
  local copies, waits for them, and re-layouts  2.11 us (7%)
  other arithmetic  1.46 us (5%)
    pallas_call x1, Pallas kernels, body(): pl.pallas_call(functools.partial(kernel, (blocks, kmax, regions)), out_sh...  28.3 us
    unnamed x1, local copies, waits for them, and re-layouts  1.28 us
    select_n x1, other arithmetic, plan(): col = jnp.where(live, tile_cols, cols).reshape(tiles)  0.69 us
    concatenate x1, local copies, waits for them, and re-layouts, plan(): return jnp.concatenate([col, tile_at, block_at, keep, last])  0.66 us

profile of v2, /device:TPU:0, one launch (start us, length us, event | category | flops | bytes accessed | tf_op | source)
XLA Modules:
  0.0 31.9 jit_solution(13858565804182983330)
XLA Ops:
  0.0 0.7 %fusion.1 = s32[16,6]{0,1:T(8,128)S(1)} fusion(s32[16,6]{0,1:T(8,128)} %param.10, s32[16]{0:T(128)} %param.11), kind=kLoop, calls=%fused_computation.14 | loop fusion | flops 192 | bytes 832 | tf_op jit(solution)/shard_map/jit(_where)/select_n | solution.py:28
  0.7 0.1 copy.12
  0.8 0.1 reshape.72
  0.9 0.1 convert_reduce_fusion.1
  1.0 0.1 select_reduce_fusion.3
  1.1 0.2 convert_reduce_fusion
  1.3 0.1 select_reduce_fusion
  1.4 0.1 select_reduce_fusion.2
  1.6 0.1 and_reduce_fusion
  1.7 0.7 %concatenate.3.lists = s32[406]{0:T(512)} concatenate(s32[96]{0:T(128)S(1)} %reshape.72, s32[116]{0:T(128)S(1)} %get-tuple-element.6, s32[116]{0:T(128)S(1)} %broadcast_add_fusion, s32[58]{0:T(128)S(1)} %convert_subtract_fusion, s32[20]{0:T(128)S(1)} %add_select_fusion), dimensions={0} | concatenate | bytes 3248 | tf_op jit(solution)/shard_map/concatenate | solution.py:46
  2.3 28.3 %shard_map.91 = f32[8,128]{1,0:T(8,128)} custom-call(s32[406]{0:T(512)} %concatenate.3.lists, s32[4,128]{1,0:T(4,128)} %bitcast.10, f32[16,128]{1,0:T(8,128)} %bitcast.9, s32[1,128]{1,0:T(1,128)} %bitcast.11, s32[64,128]{1,0:T(8,128)} %bitcast.7, bf16[96,128,128]{2,1,0:T(8,128)(2,1)} %bitcast.6, bf16[2048,128]{1,0:T(8,128)(2,1)} %init_hbm.1, ...), custom_call_target="tpu_custom_call" | custom-call | tf_op jit(solution)/shard_map/pallas_call | solution.py:338
  30.7 1.3 %copy.14 = f32[1024]{0:T(1024)} copy(f32[1024]{0:T(1024)} %bitcast.8) | data formatting | bytes 8192
  (7 shorter events, 0.1 us)

commit v3 on v2

--- a/solution.py
+++ b/solution.py
@@ -8,6 +8,7 @@
 from jax.sharding import PartitionSpec as P
 
 OFFSETS = (-2, -1, 1, 2)
+ORDER = (1, 2, 0, 3)
 MESH = pl.DeviceIdType.MESH
 F32 = jnp.float32
 BF16 = jnp.bfloat16
@@ -23,32 +24,46 @@
 
 def plan(tile_cols, tile_count):
     blocks, kmax = tile_cols.shape
+    tiles, cols, _ = dims(blocks, kmax)
+    live = lax.broadcasted_iota(jnp.int32, (blocks, kmax), 1) < tile_count[:, None]
+    col = jnp.where(live, tile_cols, cols).reshape(1, tiles)
+    return jnp.pad(col, ((0, 0), (0, 128 - tiles)), constant_values=cols)
+
+
+def make_lists(col, row, lane, shape):
+    blocks, kmax = shape
     tiles, cols, pairs = dims(blocks, kmax)
-    live = lax.broadcasted_iota(jnp.int32, (blocks, kmax), 1) < tile_count[:, None]
-    col = jnp.where(live, tile_cols, cols).reshape(tiles)
-    tile = jnp.arange(tiles, dtype=jnp.int32)
-    cid = jnp.arange(cols, dtype=jnp.int32)
-    same = col[:, None] == col[None, :]
-    rank = jnp.sum((same & (tile[None, :] < tile[:, None])).astype(jnp.int32), 1)
-    count = jnp.sum((col[:, None] == cid[None, :]).astype(jnp.int32), 0)
-    padded = (count + 1) // 2 * 2
-    start = jnp.sum(jnp.where(cid[None, :] < cid[:, None], padded[None, :], 0), 1)
-    first = jnp.sum(jnp.where(cid[None, :] < col[:, None], padded[None, :], 0), 1)
+
+    def down(x):
+        return jnp.sum(x, axis=0, keepdims=True)
+
+    def across(x):
+        return jnp.sum(x, axis=1, keepdims=True)
+
+    col = jnp.where(lane[:1] < tiles, col, cols)
+    by_lane = jnp.broadcast_to(col, row.shape)
+    by_row = by_lane.T
+    rank = down(jnp.where((by_lane == by_row) & (row < lane), 1, 0))
+    count_row = down(jnp.where((by_row == lane) & (lane < cols), 1, 0))
+    count_col = across(jnp.where((by_lane == row) & (row < cols), 1, 0))
+    padded_row = jnp.bitwise_and(count_row + 1, -2)
+    padded_col = jnp.bitwise_and(count_col + 1, -2)
+    start_row = down(jnp.where(row < lane, padded_col, 0))
+    start_col = across(jnp.where(lane < row, padded_row, 0))
+    first = down(jnp.where(row < by_lane, padded_col, 0))
     spot = jnp.where(col < cols, first + rank, -1)
-    slot = jnp.arange(2 * pairs, dtype=jnp.int32)
-    hit = slot[:, None] == spot[None, :]
-    tile_at = jnp.sum(jnp.where(hit, tile[None, :], 0), 1)
-    block_at = blocks + jnp.sum(jnp.where(hit, (tile // kmax - blocks)[None, :], 0), 1)
-    pair = jnp.arange(pairs, dtype=jnp.int32)
-    fresh = jnp.any((pair[:, None] * 2 == start[None, :]) & (count[None, :] > 0), 1)
-    keep = 1 - fresh.astype(jnp.int32)
-    last = jnp.where(count > 0, (start + padded) // 2 - 1, pairs)
-    return jnp.concatenate([col, tile_at, block_at, keep, last])
+    hit = jnp.broadcast_to(spot, row.shape).T == lane
+    tile_at = down(jnp.where(hit, row, 0))
+    owner = lax.shift_right_logical(row * (256 // kmax + 1), 8)
+    block_at = blocks + down(jnp.where(hit, owner - blocks, 0))
+    keep = 1 - down(jnp.where((start_col == 2 * lane) & (count_col > 0), 1, 0))
+    last = jnp.where(count_row > 0, lax.shift_right_logical(start_row + padded_row, 1) - 1, pairs)
+    return jnp.concatenate([col, tile_at, block_at, keep, last, col, col, col], 0)
 
 
 def kernel(
     shape,
-    lists,
+    columns,
     publish,
     reward,
     goal,
@@ -72,15 +87,19 @@
     flow_u,
     sums,
     part1,
-    part2,
     arr1,
-    arr2,
     total,
     other,
+    terms,
+    away,
+    table,
+    lists,
     load_sem,
     send_sem,
     recv_sem,
     dest_sem,
+    terms_send,
+    terms_recv,
 ):
     blocks, kmax, regions = shape
     tiles, cols, pairs = dims(blocks, kmax)
@@ -88,9 +107,7 @@
     me = lax.axis_index("region")
     side = lax.axis_index("dest")
     first_seg = me * (blocks * tile)
-    at_tile, at_block = tiles, tiles + 2 * pairs
-    at_keep = tiles + 4 * pairs
-    at_last = at_keep + pairs
+    of_col, of_tile, of_block, of_keep, of_last = range(5)
 
     load_init = pltpu.make_async_copy(init_hbm, init, load_sem.at[0])
     load_trans = pltpu.make_async_copy(trans_hbm, trans, load_sem.at[1])
@@ -107,7 +124,8 @@
     for by in OFFSETS:
         @pl.when(inside(by))
         def _():
-            pl.semaphore_signal(barrier, inc=1, device_id={"region": me + by}, device_id_type=MESH)
+            for d in range(2):
+                pl.semaphore_signal(barrier, inc=1, device_id={"region": me + by, "dest": d}, device_id_type=MESH)
 
     zero = jnp.zeros((tile, tile), BF16)
     ext1[cols] = zero
@@ -123,7 +141,8 @@
         @pl.when(jnp.logical_not(inside(-by)))
         def _():
             arr1[j] = zero
-            arr2[j] = zero
+            for d in range(2):
+                away[d, j] = jnp.zeros((8, tile), F32)
 
     row = lax.broadcasted_iota(jnp.int32, (tile, tile), 0)
     lane = lax.broadcasted_iota(jnp.int32, (tile, tile), 1)
@@ -178,13 +197,13 @@
 
     def publish_rows(ext, piece, start):
         whole = jnp.concatenate([ext[b] for b in range(blocks)], 1)
-        for j in range(4):
+        for j in ORDER:
             picked = jnp.dot(whole, hot[j], preferred_element_type=F32)
             piece[j] = picked.astype(BF16)
             start(j)
 
     def product(ext, b):
-        left = jnp.concatenate([ext[lists[b * kmax + k]] for k in range(kmax)], 1)
+        left = jnp.concatenate([ext[lists[of_col, b * kmax + k]] for k in range(kmax)], 1)
         right = jnp.concatenate([trans[b * kmax + k] for k in range(kmax)], 1)
         return lax.dot_general(left, right, LAST, preferred_element_type=F32)
 
@@ -193,13 +212,12 @@
 
     neighbours = 1
     for by in OFFSETS:
-        neighbours = neighbours + inside(by).astype(jnp.int32)
+        neighbours = neighbours + 2 * inside(by).astype(jnp.int32)
     pl.semaphore_wait(barrier, neighbours)
 
     start1, wait1, finish1 = exchange(0, piece1, ext1, blocks, -1)
     start2, wait2, finish2 = exchange(1, piece2, ext2, blocks, -1)
     start3, wait3, finish3 = exchange(2, part1, arr1, 0, 1)
-    start4, wait4, finish4 = exchange(3, part2, arr2, 0, 1)
 
     publish_rows(ext1, piece1, start1)
 
@@ -219,8 +237,12 @@
             jnp.concatenate(highs, 1), jnp.concatenate(lows, 1), LAST, preferred_element_type=F32
         )
 
-    total[...] = lax.fori_loop(0, ids.shape[0] // group, count, jnp.zeros((blocks, tile), F32), unroll=True)
-
+    table[...] = make_lists(columns[...], row, lane, (blocks, kmax))
+    load_lists = pltpu.make_async_copy(table, lists, load_sem.at[3])
+    load_lists.start()
+    groups = ids.shape[0] // group
+    counted = lax.fori_loop(0, groups // 2, count, jnp.zeros((blocks, tile), F32), unroll=True)
+    load_lists.wait()
     load_trans.wait()
     wait1()
 
@@ -239,6 +261,7 @@
         return carry
 
     lax.fori_loop(0, blocks, turn, 0, unroll=True)
+    total[...] = lax.fori_loop(groups // 2, groups, count, counted, unroll=True)
     wait2()
 
     def second_backup(b, carry):
@@ -250,31 +273,31 @@
 
     lax.fori_loop(0, blocks, second_backup, 0, unroll=True)
 
-    def spread(part, start):
+    def spread():
         def step(t, acc):
             left = jnp.concatenate(
-                [flow_u[lists[at_block + 2 * t + h]] for h in range(2)], 1
+                [flow_u[lists[of_block, 2 * t + h]] for h in range(2)], 1
             )
-            right = jnp.concatenate([trans[lists[at_tile + 2 * t + h]] for h in range(2)], 0)
+            right = jnp.concatenate([trans[lists[of_tile, 2 * t + h]] for h in range(2)], 0)
             new = jnp.dot(left, right, preferred_element_type=F32)
-            acc = acc * lists[at_keep + t].astype(F32) + new
+            acc = acc * lists[of_keep, t].astype(F32) + new
             sums[t] = acc
             return acc
 
         lax.fori_loop(0, pairs, step, jnp.zeros((tile, tile), F32), unroll=True)
-        for j in range(4):
-            part[j] = sums[lists[at_last + blocks + j]].astype(BF16)
-            start(j)
 
     def arrive(arr, c):
         left = jnp.concatenate([arr[j] for j in range(4)], 1)
         rows = pl.ds(pl.multiple_of(c * tile, tile), tile)
         right = jnp.concatenate([hot[j, rows, :] for j in range(4)], 1)
         back = lax.dot_general(left, right, LAST, preferred_element_type=F32)
-        local = sums[lists[at_last + c]] + back
+        local = sums[lists[of_last, c]] + back
         return anchor[c] + ext2[c].astype(F32) * local
 
-    spread(part1, start3)
+    spread()
+    for j in ORDER:
+        part1[j] = sums[lists[of_last, blocks + j]].astype(BF16)
+        start3(j)
     wait3()
 
     def first_flow(c, carry):
@@ -285,11 +308,29 @@
         return carry
 
     lax.fori_loop(0, blocks, first_flow, 0, unroll=True)
-    spread(part2, start4)
-    wait4()
+    spread()
+
+    def term_copy(j, d, slot):
+        return pltpu.make_async_remote_copy(
+            src_ref=terms.at[j],
+            dst_ref=away.at[slot, j],
+            send_sem=terms_send.at[d, j],
+            recv_sem=terms_recv.at[slot, j],
+            device_id={"region": me + OFFSETS[j], "dest": d},
+            device_id_type=MESH,
+        )
+
+    for j in ORDER:
+        flow = sums[lists[of_last, blocks + j]] * ext2[blocks + j].astype(F32)
+        terms[j] = jnp.sum(flow.reshape(tile // 8, 8, tile), axis=0)
+
+        @pl.when(inside(OFFSETS[j]))
+        def _():
+            for d in range(2):
+                term_copy(j, d, side).start()
 
     def second_flow(c, carry):
-        flow = arrive(arr2, c)
+        flow = anchor[c] + ext2[c].astype(F32) * sums[lists[of_last, c]]
         here = pl.ds(c, 1)
         total[here, :] = total[here, :] - jnp.sum(flow, axis=0, keepdims=True)
         return carry
@@ -311,9 +352,32 @@
     finish1()
     finish2()
     finish3()
-    finish4()
+    for j in range(4):
+        @pl.when(inside(OFFSETS[j]))
+        def _():
+            for d in range(2):
+                term_copy(j, d, side).wait_send()
+
+        @pl.when(inside(-OFFSETS[j]))
+        def _():
+            for d in range(2):
+                term_copy(j, d, d).wait_recv()
+
+    whole = jnp.concatenate([away[0, j] + away[1, j] for j in range(4)], 1)
+    high = whole.astype(BF16)
+    rest = whole - high.astype(F32)
+    middle = rest.astype(BF16)
+    low = (rest - middle.astype(F32)).astype(BF16)
+    left = jnp.concatenate([high, middle, low, jnp.zeros_like(low)], 0)
+    lines = []
+    for i in range(share):
+        rows = pl.ds(pl.multiple_of((side * share + i) * tile, tile), tile)
+        right = jnp.concatenate([hot[j, rows, :] for j in range(4)], 1)
+        back = lax.dot_general(left, right, LAST, preferred_element_type=F32)
+        lines.append(jnp.sum(back, axis=0, keepdims=True))
+    landed = jnp.concatenate(lines, 0)
     swap.wait()
-    out[...] = total[mine, :] + other[...]
+    out[...] = total[mine, :] + other[...] - landed
 
 
 def body(
@@ -331,14 +395,13 @@
     blocks, kmax, tile, _ = transitions.shape
     width = anchor.shape[1]
     tiles, cols, pairs = dims(blocks, kmax)
-    lists = plan(tile_cols, tile_count)
+    columns = plan(tile_cols, tile_count)
     vmem = pl.BlockSpec(memory_space=pltpu.VMEM)
-    smem = pl.BlockSpec(memory_space=pltpu.SMEM)
     hbm = pl.BlockSpec(memory_space=pltpu.HBM)
     out = pl.pallas_call(
         functools.partial(kernel, (blocks, kmax, regions)),
         out_shape=jax.ShapeDtypeStruct((blocks // 2, tile), F32),
-        in_specs=[smem, vmem, vmem, vmem, vmem, hbm, hbm, hbm],
+        in_specs=[vmem, vmem, vmem, vmem, vmem, hbm, hbm, hbm],
         out_specs=vmem,
         scratch_shapes=[
             pltpu.VMEM((tiles, tile, tile), BF16),
@@ -357,20 +420,24 @@
             pltpu.VMEM((pairs + 1, width, tile), F32),
             pltpu.VMEM((4, width, tile), BF16),
             pltpu.VMEM((4, width, tile), BF16),
-            pltpu.VMEM((4, width, tile), BF16),
-            pltpu.VMEM((4, width, tile), BF16),
             pltpu.VMEM((blocks, tile), F32),
             pltpu.VMEM((blocks // 2, tile), F32),
-            pltpu.SemaphoreType.DMA((3,)),
-            pltpu.SemaphoreType.DMA((4, 4)),
-            pltpu.SemaphoreType.DMA((4, 4)),
+            pltpu.VMEM((4, 8, tile), F32),
+            pltpu.VMEM((2, 4, 8, tile), F32),
+            pltpu.VMEM((8, 128), jnp.int32),
+            pltpu.SMEM((8, 128), jnp.int32),
+            pltpu.SemaphoreType.DMA((4,)),
+            pltpu.SemaphoreType.DMA((3, 4)),
+            pltpu.SemaphoreType.DMA((3, 4)),
             pltpu.SemaphoreType.DMA((2,)),
+            pltpu.SemaphoreType.DMA((2, 4)),
+            pltpu.SemaphoreType.DMA((2, 4)),
         ],
         compiler_params=pltpu.CompilerParams(
             collective_id=0, has_side_effects=True, vmem_limit_bytes=56 * 1024 * 1024
         ),
     )(
-        lists,
+        columns,
         publish[0],
         reward.reshape(blocks, tile),
         goal_segment_index.reshape(1, width),

time: 32.2 us -> 29.7 us (0.922)
  Pallas kernels: 28.3 us -> 26.8 us
  other arithmetic: 1.46 us -> 0.69 us
    pallas_call x1, Pallas kernels: 28.3 us -> 26.8 us  [body(): pl.pallas_call(functools.partial(kernel, (blocks, kmax, regions)), out_sh...]
    concatenate x1 -> x0, local copies, waits for them, and re-layouts: 0.66 us -> none  [plan(): return jnp.concatenate([col, tile_at, block_at, keep, last])]
    reduce_sum x5 -> x0, other arithmetic: 0.6 us -> none  [the longest x1 0.17 us: plan(): jnp.sum((same & (tile[None, :] < tile[:, None])).astype(jnp.int32), 1)]
    pad x0 -> x1, local copies, waits for them, and re-layouts: none -> 0.52 us  [plan(): return jnp.pad(col, ((0, 0), (0, 128 - tiles)), constant_values=cols)]
    select_n x3 -> x1, other arithmetic: 0.73 us -> 0.69 us  [plan(): col = jnp.where(live, tile_cols, cols).reshape(1, tiles)]
where the time goes in v3:
time: 29.7 us; the launch traced here: 29.5 us
  Pallas kernels  26.8 us (90%)
  local copies, waits for them, and re-layouts  1.97 us (7%)
  other arithmetic  0.69 us (2%)
    pallas_call x1, Pallas kernels, body(): pl.pallas_call(functools.partial(kernel, (blocks, kmax, regions)), out_sh...  26.8 us
    unnamed x1, local copies, waits for them, and re-layouts  1.28 us
    select_n x1, other arithmetic, plan(): col = jnp.where(live, tile_cols, cols).reshape(1, tiles)  0.69 us

profile of v3, /device:TPU:0, one launch (start us, length us, event | category | flops | bytes accessed | tf_op | source)
XLA Modules:
  0.0 29.5 jit_solution(15112250756069999577)
XLA Ops:
  0.0 0.7 %fusion = s32[16,6]{0,1:T(8,128)S(1)} fusion(s32[16,6]{0,1:T(8,128)} %param.10, s32[16]{0:T(128)} %param.11), kind=kLoop, calls=%fused_computation.1 | loop fusion | flops 192 | bytes 832 | tf_op jit(solution)/shard_map/jit(_where)/select_n | solution.py:29
  0.7 0.1 copy.11
  0.8 0.1 reshape.16
  0.9 0.5 %pad.4.columns = s32[1,128]{1,0:T(1,128)} pad(s32[1,96]{1,0:T(1,128)S(1)} %reshape.16, s32[]{:T(128)} %constant.0.clone.1), padding=0_0x0_32 | pad | bytes 900 | tf_op jit(solution)/shard_map/jit(_pad)/pad | solution.py:30
  1.4 26.8 %shard_map.91 = f32[8,128]{1,0:T(8,128)} custom-call(s32[1,128]{1,0:T(1,128)} %pad.4.columns, s32[4,128]{1,0:T(4,128)} %bitcast.10, f32[16,128]{1,0:T(8,128)} %bitcast.9, s32[1,128]{1,0:T(1,128)} %bitcast.11, s32[64,128]{1,0:T(8,128)} %bitcast.7, bf16[96,128,128]{2,1,0:T(8,128)(2,1)} %bitcast.6, bf16[2048,128]{1,0:T(8,128)(2,1)} %init_hbm.1, ...), custom_call_target="tpu_custom_call" | custom-call | tf_op jit(solution)/shard_map/pallas_call | solution.py:401
  28.2 1.3 %copy.13 = f32[1024]{0:T(1024)} copy(f32[1024]{0:T(1024)} %bitcast.8) | data formatting | bytes 8192

commit v4 on v3

--- a/solution.py
+++ b/solution.py
@@ -72,6 +72,7 @@
     init_hbm,
     anchor_hbm,
     out,
+    out_less,
     trans,
     init,
     anchor_in,
@@ -377,7 +378,8 @@
         lines.append(jnp.sum(back, axis=0, keepdims=True))
     landed = jnp.concatenate(lines, 0)
     swap.wait()
-    out[...] = total[mine, :] + other[...] - landed
+    out[...] = total[mine, :] + other[...]
+    out_less[...] = landed
 
 
 def body(
@@ -398,11 +400,11 @@
     columns = plan(tile_cols, tile_count)
     vmem = pl.BlockSpec(memory_space=pltpu.VMEM)
     hbm = pl.BlockSpec(memory_space=pltpu.HBM)
-    out = pl.pallas_call(
+    out, less = pl.pallas_call(
         functools.partial(kernel, (blocks, kmax, regions)),
-        out_shape=jax.ShapeDtypeStruct((blocks // 2, tile), F32),
+        out_shape=[jax.ShapeDtypeStruct((blocks // 2, tile), F32)] * 2,
         in_specs=[vmem, vmem, vmem, vmem, vmem, hbm, hbm, hbm],
-        out_specs=vmem,
+        out_specs=[vmem, vmem],
         scratch_shapes=[
             pltpu.VMEM((tiles, tile, tile), BF16),
             pltpu.VMEM((blocks * tile, width), BF16),
@@ -446,7 +448,7 @@
         value_init,
         anchor,
     )
-    return out.reshape(-1)
+    return (out - less).reshape(-1)
 
 
 def solution(mesh):

time: 29.7 us -> 29.8 us (level)
  other arithmetic: 0.69 us -> 1.99 us
  local copies, waits for them, and re-layouts: 1.97 us -> 0.69 us
    reshape x0 -> x1, other arithmetic: none -> 1.29 us  [body(): return (out - less).reshape(-1)]
    unnamed x1 -> x0, local copies, waits for them, and re-layouts: 1.28 us -> none
where the time goes in v4:
time: 29.8 us; the launch traced here: 29.5 us
  Pallas kernels  26.8 us (90%)
  other arithmetic  1.99 us (7%)
  local copies, waits for them, and re-layouts  0.69 us (2%)
    pallas_call x1, Pallas kernels, body(): pl.pallas_call(functools.partial(kernel, (blocks, kmax, regions)), out_sh...  26.8 us
    reshape x1, other arithmetic, body(): return (out - less).reshape(-1)  1.29 us
    select_n x1, other arithmetic, plan(): col = jnp.where(live, tile_cols, cols).reshape(1, tiles)  0.69 us

profile of v4, /device:TPU:0, one launch (start us, length us, event | category | flops | bytes accessed | tf_op | source)
XLA Modules:
  0.0 29.5 jit_solution(14845300869242015891)
XLA Ops:
  0.0 0.7 %fusion = s32[16,6]{0,1:T(8,128)S(1)} fusion(s32[16,6]{0,1:T(8,128)} %param.10, s32[16]{0:T(128)} %param.11), kind=kLoop, calls=%fused_computation.2 | loop fusion | flops 192 | bytes 832 | tf_op jit(solution)/shard_map/jit(_where)/select_n | solution.py:29
  0.7 0.1 copy.11
  0.8 0.1 reshape.16
  0.9 0.5 %pad.4.columns = s32[1,128]{1,0:T(1,128)} pad(s32[1,96]{1,0:T(1,128)S(1)} %reshape.16, s32[]{:T(128)} %constant.0.clone.1), padding=0_0x0_32 | pad | bytes 900 | tf_op jit(solution)/shard_map/jit(_pad)/pad | solution.py:30
  1.4 26.8 %shard_map.91 = (f32[8,128]{1,0:T(8,128)}, f32[8,128]{1,0:T(8,128)}) custom-call(s32[1,128]{1,0:T(1,128)} %pad.4.columns, s32[4,128]{1,0:T(4,128)} %bitcast.10, f32[16,128]{1,0:T(8,128)} %bitcast.9, s32[1,128]{1,0:T(1,128)} %bitcast.11, s32[64,128]{1,0:T(8,128)} %bitcast.8, bf16[96,128,128]{2,1,0:T(8,128)(2,1)} %bitcast.7, bf16[2048,128]{1,0:T(8,128)(2,1)} %init_hbm.1, ...), custom_call_target="tpu_custom_call" | custom-call | tf_op jit(solution)/shard_map/pallas_call | solution.py:403
  28.2 1.3 %subtract_bitcast_fusion = f32[1024]{0:T(1024)} fusion(f32[8,128]{1,0:T(8,128)} %get-tuple-element.7, f32[8,128]{1,0:T(8,128)} %get-tuple-element.8), kind=kLoop, calls=%fused_computation | loop fusion | flops 1024 | bytes 12288 | tf_op jit(solution)/shard_map/reshape | solution.py:451

commit v5 on v3

--- a/solution.py
+++ b/solution.py
@@ -41,6 +41,9 @@
         return jnp.sum(x, axis=1, keepdims=True)
 
     col = jnp.where(lane[:1] < tiles, col, cols)
+    def order(c):
+        return jnp.where(c >= blocks, c - blocks, c + 4)
+
     by_lane = jnp.broadcast_to(col, row.shape)
     by_row = by_lane.T
     rank = down(jnp.where((by_lane == by_row) & (row < lane), 1, 0))
@@ -48,9 +51,9 @@
     count_col = across(jnp.where((by_lane == row) & (row < cols), 1, 0))
     padded_row = jnp.bitwise_and(count_row + 1, -2)
     padded_col = jnp.bitwise_and(count_col + 1, -2)
-    start_row = down(jnp.where(row < lane, padded_col, 0))
-    start_col = across(jnp.where(lane < row, padded_row, 0))
-    first = down(jnp.where(row < by_lane, padded_col, 0))
+    start_row = down(jnp.where(order(row) < order(lane), padded_col, 0))
+    start_col = across(jnp.where(order(lane) < order(row), padded_row, 0))
+    first = down(jnp.where(order(row) < order(by_lane), padded_col, 0))
     spot = jnp.where(col < cols, first + rank, -1)
     hit = jnp.broadcast_to(spot, row.shape).T == lane
     tile_at = down(jnp.where(hit, row, 0))
@@ -256,12 +259,16 @@
 
     load_anchor.wait()
 
+    total[...] = lax.fori_loop(groups // 2, groups, count, counted, unroll=True)
+
     def turn(b, carry):
-        anchor[b] = anchor_in[pl.ds(pl.multiple_of(b * tile, tile), tile), :].astype(F32).T
+        block = anchor_in[pl.ds(pl.multiple_of(b * tile, tile), tile), :].astype(F32).T
+        anchor[b] = block
+        here = pl.ds(b, 1)
+        total[here, :] = total[here, :] - 2.0 * jnp.sum(block, axis=0, keepdims=True)
         return carry
 
     lax.fori_loop(0, blocks, turn, 0, unroll=True)
-    total[...] = lax.fori_loop(groups // 2, groups, count, counted, unroll=True)
     wait2()
 
     def second_backup(b, carry):
@@ -273,7 +280,9 @@
 
     lax.fori_loop(0, blocks, second_backup, 0, unroll=True)
 
-    def spread():
+    early = min(((kmax - 1) * blocks + 4) // 2, pairs)
+
+    def spread(low, high, acc):
         def step(t, acc):
             left = jnp.concatenate(
                 [flow_u[lists[of_block, 2 * t + h]] for h in range(2)], 1
@@ -284,31 +293,38 @@
             sums[t] = acc
             return acc
 
-        lax.fori_loop(0, pairs, step, jnp.zeros((tile, tile), F32), unroll=True)
+        return lax.fori_loop(low, high, step, acc, unroll=True)
 
     def arrive(arr, c):
         left = jnp.concatenate([arr[j] for j in range(4)], 1)
         rows = pl.ds(pl.multiple_of(c * tile, tile), tile)
         right = jnp.concatenate([hot[j, rows, :] for j in range(4)], 1)
         back = lax.dot_general(left, right, LAST, preferred_element_type=F32)
-        local = sums[lists[of_last, c]] + back
-        return anchor[c] + ext2[c].astype(F32) * local
-
-    spread()
+        return anchor[c] + ext2[c].astype(F32) * back
+
+    none = jnp.zeros((tile, tile), F32)
+    acc = spread(0, early, none)
     for j in ORDER:
         part1[j] = sums[lists[of_last, blocks + j]].astype(BF16)
         start3(j)
+    spread(early, pairs, acc)
+
+    def local_flow(c, carry):
+        anchor[c] = anchor[c] + ext2[c].astype(F32) * sums[lists[of_last, c]]
+        return carry
+
+    lax.fori_loop(0, blocks, local_flow, 0, unroll=True)
     wait3()
 
     def first_flow(c, carry):
         flow = arrive(arr1, c)
         flow_u[c] = (flow * inv[c]).astype(BF16)
         here = pl.ds(c, 1)
-        total[here, :] = total[here, :] - jnp.sum(anchor[c] + flow, axis=0, keepdims=True)
+        total[here, :] = total[here, :] - jnp.sum(flow, axis=0, keepdims=True)
         return carry
 
     lax.fori_loop(0, blocks, first_flow, 0, unroll=True)
-    spread()
+    acc = spread(0, early, none)
 
     def term_copy(j, d, slot):
         return pltpu.make_async_remote_copy(
@@ -329,8 +345,10 @@
             for d in range(2):
                 term_copy(j, d, side).start()
 
+    spread(early, pairs, acc)
+
     def second_flow(c, carry):
-        flow = anchor[c] + ext2[c].astype(F32) * sums[lists[of_last, c]]
+        flow = ext2[c].astype(F32) * sums[lists[of_last, c]]
         here = pl.ds(c, 1)
         total[here, :] = total[here, :] - jnp.sum(flow, axis=0, keepdims=True)
         return carry

time: 29.7 us -> 29.1 us (0.980)
  Pallas kernels: 26.8 us -> 26.2 us
    pallas_call x1, Pallas kernels: 26.8 us -> 26.2 us  [body(): pl.pallas_call(functools.partial(kernel, (blocks, kmax, regions)), out_sh...]
where the time goes in v5:
time: 29.1 us; the launch traced here: 28.9 us
  Pallas kernels  26.2 us (90%)
  local copies, waits for them, and re-layouts  1.97 us (7%)
  other arithmetic  0.69 us (2%)
    pallas_call x1, Pallas kernels, body(): pl.pallas_call(functools.partial(kernel, (blocks, kmax, regions)), out_sh...  26.2 us
    unnamed x1, local copies, waits for them, and re-layouts  1.28 us
    select_n x1, other arithmetic, plan(): col = jnp.where(live, tile_cols, cols).reshape(1, tiles)  0.69 us

profile of v5, /device:TPU:0, one launch (start us, length us, event | category | flops | bytes accessed | tf_op | source)
XLA Modules:
  0.0 28.9 jit_solution(17480968493667371548)
XLA Ops:
  0.0 0.7 %fusion = s32[16,6]{0,1:T(8,128)S(1)} fusion(s32[16,6]{0,1:T(8,128)} %param.10, s32[16]{0:T(128)} %param.11), kind=kLoop, calls=%fused_computation.1 | loop fusion | flops 192 | bytes 832 | tf_op jit(solution)/shard_map/jit(_where)/select_n | solution.py:29
  0.7 0.1 copy.11
  0.8 0.1 reshape.16
  0.9 0.5 %pad.4.columns = s32[1,128]{1,0:T(1,128)} pad(s32[1,96]{1,0:T(1,128)S(1)} %reshape.16, s32[]{:T(128)} %constant.0.clone.1), padding=0_0x0_32 | pad | bytes 900 | tf_op jit(solution)/shard_map/jit(_pad)/pad | solution.py:30
  1.4 26.2 %shard_map.91 = f32[8,128]{1,0:T(8,128)} custom-call(s32[1,128]{1,0:T(1,128)} %pad.4.columns, s32[4,128]{1,0:T(4,128)} %bitcast.10, f32[16,128]{1,0:T(8,128)} %bitcast.9, s32[1,128]{1,0:T(1,128)} %bitcast.11, s32[64,128]{1,0:T(8,128)} %bitcast.7, bf16[96,128,128]{2,1,0:T(8,128)(2,1)} %bitcast.6, bf16[2048,128]{1,0:T(8,128)(2,1)} %init_hbm.1, ...), custom_call_target="tpu_custom_call" | custom-call | tf_op jit(solution)/shard_map/pallas_call | solution.py:419
  27.6 1.3 %copy.13 = f32[1024]{0:T(1024)} copy(f32[1024]{0:T(1024)} %bitcast.8) | data formatting | bytes 8192

commit v6 on v5

--- a/solution.py
+++ b/solution.py
@@ -22,15 +22,7 @@
     return tiles, cols, pairs
 
 
-def plan(tile_cols, tile_count):
-    blocks, kmax = tile_cols.shape
-    tiles, cols, _ = dims(blocks, kmax)
-    live = lax.broadcasted_iota(jnp.int32, (blocks, kmax), 1) < tile_count[:, None]
-    col = jnp.where(live, tile_cols, cols).reshape(1, tiles)
-    return jnp.pad(col, ((0, 0), (0, 128 - tiles)), constant_values=cols)
-
-
-def make_lists(col, row, lane, shape):
+def make_lists(tile_cols, tile_count, row, lane, shape):
     blocks, kmax = shape
     tiles, cols, pairs = dims(blocks, kmax)
 
@@ -40,12 +32,25 @@
     def across(x):
         return jnp.sum(x, axis=1, keepdims=True)
 
-    col = jnp.where(lane[:1] < tiles, col, cols)
+    def grid(width, dim):
+        return lax.broadcasted_iota(jnp.int32, (row.shape[0], width), dim)
+
+    def owner_of(p):
+        return lax.shift_right_logical(p * (256 // kmax + 1), 8)
+
+    place = owner_of(grid(kmax, 0))
+    turn = grid(kmax, 0) - place * kmax
+    cells = jnp.zeros(place.shape, jnp.int32)
+    for b in range(blocks):
+        cells = jnp.where(place == b, tile_cols[b : b + 1, :], cells)
+    cell = across(jnp.where(grid(kmax, 1) == turn, cells, 0))
+    alive = across(jnp.where(grid(blocks, 1) == owner_of(grid(blocks, 0)), tile_count, 0))
+    by_row = jnp.broadcast_to(jnp.where(turn[:, :1] < alive, cell, cols), row.shape)
+    by_lane = by_row.T
+    col = by_lane[:1]
     def order(c):
         return jnp.where(c >= blocks, c - blocks, c + 4)
 
-    by_lane = jnp.broadcast_to(col, row.shape)
-    by_row = by_lane.T
     rank = down(jnp.where((by_lane == by_row) & (row < lane), 1, 0))
     count_row = down(jnp.where((by_row == lane) & (lane < cols), 1, 0))
     count_col = across(jnp.where((by_lane == row) & (row < cols), 1, 0))
@@ -57,7 +62,7 @@
     spot = jnp.where(col < cols, first + rank, -1)
     hit = jnp.broadcast_to(spot, row.shape).T == lane
     tile_at = down(jnp.where(hit, row, 0))
-    owner = lax.shift_right_logical(row * (256 // kmax + 1), 8)
+    owner = owner_of(row)
     block_at = blocks + down(jnp.where(hit, owner - blocks, 0))
     keep = 1 - down(jnp.where((start_col == 2 * lane) & (count_col > 0), 1, 0))
     last = jnp.where(count_row > 0, lax.shift_right_logical(start_row + padded_row, 1) - 1, pairs)
@@ -66,7 +71,8 @@
 
 def kernel(
     shape,
-    columns,
+    tile_cols,
+    tile_count,
     publish,
     reward,
     goal,
@@ -240,7 +246,7 @@
             jnp.concatenate(highs, 1), jnp.concatenate(lows, 1), LAST, preferred_element_type=F32
         )
 
-    table[...] = make_lists(columns[...], row, lane, (blocks, kmax))
+    table[...] = make_lists(tile_cols[...], tile_count[...], row, lane, (blocks, kmax))
     load_lists = pltpu.make_async_copy(table, lists, load_sem.at[3])
     load_lists.start()
     groups = ids.shape[0] // group
@@ -413,13 +419,12 @@
     blocks, kmax, tile, _ = transitions.shape
     width = anchor.shape[1]
     tiles, cols, pairs = dims(blocks, kmax)
-    columns = plan(tile_cols, tile_count)
     vmem = pl.BlockSpec(memory_space=pltpu.VMEM)
     hbm = pl.BlockSpec(memory_space=pltpu.HBM)
     out = pl.pallas_call(
         functools.partial(kernel, (blocks, kmax, regions)),
         out_shape=jax.ShapeDtypeStruct((blocks // 2, tile), F32),
-        in_specs=[vmem, vmem, vmem, vmem, vmem, hbm, hbm, hbm],
+        in_specs=[vmem, vmem, vmem, vmem, vmem, vmem, hbm, hbm, hbm],
         out_specs=vmem,
         scratch_shapes=[
             pltpu.VMEM((tiles, tile, tile), BF16),
@@ -455,7 +460,8 @@
             collective_id=0, has_side_effects=True, vmem_limit_bytes=56 * 1024 * 1024
         ),
     )(
-        columns,
+        tile_cols,
+        tile_count.reshape(1, blocks),
         publish[0],
         reward.reshape(blocks, tile),
         goal_segment_index.reshape(1, width),

time: 29.1 us -> 29.1 us (level)
  other arithmetic: 0.69 us -> 0 us
  local copies, waits for them, and re-layouts: 1.97 us -> 2.62 us
    unnamed x1 -> x2, local copies, waits for them, and re-layouts: 1.28 us -> 2.62 us
    select_n x1 -> x0, other arithmetic: 0.69 us -> none  [plan(): col = jnp.where(live, tile_cols, cols).reshape(1, tiles)]
    pad x1 -> x0, local copies, waits for them, and re-layouts: 0.52 us -> none  [plan(): return jnp.pad(col, ((0, 0), (0, 128 - tiles)), constant_values=cols)]
where the time goes in v6:
time: 29.1 us; the launch traced here: 28.8 us
  Pallas kernels  26.2 us (90%)
  local copies, waits for them, and re-layouts  2.62 us (9%)
    pallas_call x1, Pallas kernels, body(): pl.pallas_call(functools.partial(kernel, (blocks, kmax, regions)), out_sh...  26.2 us
    unnamed x2, local copies, waits for them, and re-layouts  2.62 us

profile of v6, /device:TPU:0, one launch (start us, length us, event | category | flops | bytes accessed | tf_op | source)
XLA Modules:
  0.0 28.8 jit_solution(16593641492250163539)
XLA Ops:
  0.0 1.4 %copy.10.tile_cols = s32[16,6]{1,0:T(8,128)} copy(s32[16,6]{0,1:T(8,128)} %param.10) | data formatting | bytes 768 | tf_op args[1]
  1.4 26.2 %shard_map.91 = f32[8,128]{1,0:T(8,128)} custom-call(s32[16,6]{1,0:T(8,128)} %copy.10.tile_cols, s32[1,16]{1,0:T(1,128)} %bitcast.12, s32[4,128]{1,0:T(4,128)} %bitcast.11, f32[16,128]{1,0:T(8,128)} %bitcast.10, s32[1,128]{1,0:T(1,128)} %bitcast.13, s32[64,128]{1,0:T(8,128)} %bitcast.8, bf16[96,128,128]{2,1,0:T(8,128)(2,1)} %bitcast.7, ...), custom_call_target="tpu_custom_call" | custom-call | tf_op jit(solution)/shard_map/pallas_call | solution.py:424
  27.6 1.3 %copy.12 = f32[1024]{0:T(1024)} copy(f32[1024]{0:T(1024)} %bitcast.9) | data formatting | bytes 8192
